TPU v7x, 32 devices: a whole 2x2x4 slice. The times are simulated.
32 devices in a mesh: copies: 2 (over y), blk: 4 (over x, core), virt: 4 (over z).
Axes of the slice: x: 2, y: 2, z: 4, core: 2. Of those that a mesh axis runs over, the one named last changes fastest.
Arguments:
- three_index: bfloat16 [32, 512, 2048], P(('copies', 'blk'), 'virt'), parts along dimension 0, may hold values from -0.59765625 to 0.59765625
- occ_energy: float32 [32], P(('copies', 'blk')), parts along dimension 0, may hold values from -2 to -0.5
- virt_energy: float32 [1024], P('copies'), parts along dimension 0, may hold values from 0.3 to 3
Outputs:
- gradient: bfloat16 [32, 512, 2048], P(('copies', 'blk'), 'virt'), parts along dimension 0
There are 2 independent parts, one for each index of `copies`. A program takes and returns all parts, laid end to end along the dimension named above; each array names one. Nothing has to cross between parts.
All inputs are finite; a program needn't handle non-finite values.
Results may differ from a plain program's by a relative error of at most 0.0055.
Values may be sent and summed in bfloat16 or wider, within the bound.
No kernel may reach another device: no remote copies, remote signals or barrier semaphores. Data moves between devices by JAX's collectives and lax.ppermute only.
A program may use at most 64 MiB of HBM per device.

v0:
```python
import jax
import jax.numpy as jnp
from jax import lax
from jax.sharding import PartitionSpec as P


def shifted(shard, axis, by):
    devices = lax.axis_size(axis)
    return lax.ppermute(shard, axis, [(i, (i + by) % devices) for i in range(devices)])


def contract(left, right):
    return lax.dot_general(
        left, right, (((1,), (1,)), ((), ())), preferred_element_type=jnp.float32
    )


def pair_block(
    own_rows,
    part_full,
    part_rows,
    own_full,
    energy_own,
    energy_part,
    energy_rows,
    virt_energy,
    diagonal,
):
    occ_count, rows_here, aux_count = own_rows.shape
    virt_count = part_full.shape[1]
    first = contract(
        own_rows.reshape(occ_count * rows_here, aux_count),
        part_full.reshape(occ_count * virt_count, aux_count),
    )
    first = first.reshape(occ_count, rows_here, occ_count, virt_count)
    if diagonal:
        second = first.transpose(2, 1, 0, 3)
    else:
        second = contract(
            part_rows.reshape(occ_count * rows_here, aux_count),
            own_full.reshape(occ_count * virt_count, aux_count),
        )
        second = second.reshape(occ_count, rows_here, occ_count, virt_count).transpose(2, 1, 0, 3)
    denom = (
        energy_own[:, None, None, None]
        + energy_part[None, None, :, None]
        - energy_rows[None, :, None, None]
        - virt_energy[None, None, None, :]
    )
    tbar = ((2.0 * first - second) / denom).astype(jnp.bfloat16)
    flat = tbar.reshape(occ_count * rows_here, occ_count * virt_count)
    own = jnp.dot(
        flat,
        part_full.reshape(occ_count * virt_count, aux_count),
        preferred_element_type=jnp.float32,
    )
    return (tbar, first, own.reshape(occ_count, rows_here, aux_count))


def local(three_index, occ_energy, virt_energy):
    occ_count, rows_here, aux_count = three_index.shape
    virt_count = virt_energy.shape[0]
    row_start = lax.axis_index("virt") * rows_here
    energy_rows = lax.dynamic_slice_in_dim(virt_energy, row_start, rows_here, 0)
    own_full = lax.all_gather(three_index, "virt", axis=1, tiled=True)
    part_full, energy_part = (
        shifted(own_full, "blk", 1),
        shifted(occ_energy.astype(jnp.bfloat16), "blk", 1).astype(occ_energy.dtype),
    )
    part_rows = lax.dynamic_slice_in_dim(part_full, row_start, rows_here, 1)
    unused_tbar, unused_first, diag_own = pair_block(
        three_index,
        own_full,
        three_index,
        own_full,
        occ_energy,
        occ_energy,
        energy_rows,
        virt_energy,
        True,
    )
    tbar, first, cross_own = pair_block(
        three_index,
        part_full,
        part_rows,
        own_full,
        occ_energy,
        energy_part,
        energy_rows,
        virt_energy,
        False,
    )
    tiles = lax.all_to_all(tbar, "virt", split_axis=3, concat_axis=1, tiled=True)
    partial_value = lax.dot_general(
        tiles.reshape(occ_count * virt_count, occ_count * rows_here),
        own_full.reshape(occ_count * virt_count, aux_count),
        (((0,), (0,)), ((), ())),
        preferred_element_type=jnp.float32,
    )
    summed = partial_value.reshape(occ_count, rows_here, aux_count).astype(jnp.bfloat16)
    partner = shifted(summed, "blk", -1)
    return (diag_own + cross_own + partner.astype(jnp.float32)).astype(jnp.bfloat16)


def solution(mesh):
    placed = (P(("copies", "blk"), "virt", None), P(("copies", "blk")), P("copies"))
    return jax.shard_map(
        local,
        mesh=mesh,
        in_specs=placed,
        out_specs=P(("copies", "blk"), "virt", None),
        check_vma=False,
    )
```

profile of v0, /device:TPU:1, one launch (start us, length us, event | category | flops | bytes accessed | tf_op | source)
XLA Modules:
  0.0 382.6 jit_solution(1829108738289670631)
XLA Ops:
  6.5 0.0 all-gather.2.cloned.1.call-start
  6.5 0.7 all-gather.2.cloned.1.call-update
  7.3 153.6 %all-gather.2.cloned.1.call-done = bf16[4,512,2048]{2,1,0:T(8,128)(2,1)} async-done(((bf16[4,128,2048]{2,1,0:T(8,128)(2,1)}), bf16[4,512,2048]{2,1,0:T(8,128)(2,1)}) %all-gather.2.cloned.1.call-update) | async-done | bytes 8388624 | tf_op jit(solution)/shard_map/all_gather | solution.py:65
  160.9 1.5 collective-permute-start
  162.4 0.7 convert_element_type.22
  163.1 0.1 collective-permute-start.1
  163.1 0.8 dynamic_slice.6
  163.9 89.2 %collective-permute-done.1 = bf16[4]{0:T(256)(128)(2,1)S(1)} collective-permute-done((bf16[4]{0:T(256)(128)(2,1)S(1)}, bf16[4]{0:T(256)(128)(2,1)S(1)}, u32[]{:S(2)}, u32[]{:S(2)}) %collective-permute-start.1) | collective-permute-done | bytes 40 | tf_op jit(solution)/shard_map/ppermute | solution.py:9
  253.1 0.8 broadcast_add_fusion
  253.9 0.0 slice-start
  253.9 0.1 broadcast_subtract_fusion
  254.0 0.0 slice-start.1
  254.0 0.0 copy-start.3
  254.0 0.0 collective-permute-done
  254.0 7.9 %fusion.2 = f32[4,128,4,512]{3,1,0,2:T(8,128)S(1)} fusion(bf16[4,512,2048]{2,1,0:T(8,128)(2,1)} %collective-permute-done, bf16[4,128,2048]{2,1,0:T(8,128)(2,1)} %param.3), kind=kOutput, calls=%fused_computation.2 | convolution fusion | flops 4294967296 | bytes 14680064 | tf_op jit(solution)/shard_map/dot_general | solution.py:13
  261.9 0.0 slice-done
  261.9 0.0 slice-done.1
  261.9 0.0 copy-done.3
  262.0 6.9 %fusion.13 = bf16[4,128,4,512]{3,1,0,2:T(8,128)(2,1)S(1)} fusion(f32[4,128,4,512]{3,1,0,2:T(8,128)S(1)} %fusion.2, bf16[4,512,2048]{2,1,0:T(8,128)(2,1)S(1)} %bitcast.76, f32[4,128,4]{1,0,2:T(4,128)S(1)} %get-tuple-element.5, bf16[4,512,2048]{2,1,0:T(8,128)(2,1)} %collective-permute-done, s32[]{:T(128)S(6)} %select_n.4, f32[512]{0:T(512)S(1)} %copy-done.3), kind=kOutput, calls=%fused_computation.15 | convolution fusion | flops 4300210176 | bytes 16787460 | tf_op jit(solution)/shard_map/dot_general | solution.py:13
  268.9 0.0 copy-start.1
  268.9 1.3 copy-done.1
  270.2 3.1 copy.16
  273.3 50.8 %all_to_all.15 = bf16[4,128,4,512]{1,0,2,3:T(4,128)(2,1)S(1)} all-to-all(bf16[4,128,4,512]{1,0,2,3:T(4,128)(2,1)} %copy.16), channel_id=1, replica_groups=mesh['copies'=2,'blk'=4,'virt'=4] {'virt'}, dimensions={3} | all-to-all | bytes 4194304 | tf_op jit(solution)/shard_map/all_to_all | solution.py:93
  324.1 3.1 copy.17
  327.2 2.0 copy.30
  329.1 2.4 copy.18
  331.5 0.0 copy-start
  331.5 8.7 %convolution_convert_fusion = bf16[4,128,2048]{2,1,0:T(8,128)(2,1)S(1)} fusion(bf16[4,128,2048]{2,1,0:T(8,128)(2,1)} %bitcast.73, bf16[2048,2048,1]{1,0,2:T(8,128)(2,1)} %bitcast.74), kind=kOutput, calls=%fused_computation.20 | convolution fusion | flops 4296015872 | bytes 12582912 | tf_op jit(solution)/shard_map/dot_general | solution.py:94
  340.2 2.1 collective-permute-start.2
  342.3 0.0 copy-done
  342.3 6.9 %fusion.8 = f32[4,128,4,512]{3,1,2,0:T(8,128)S(1)} fusion(bf16[4,512,2048]{2,1,0:T(8,128)(2,1)} %all-gather.2.cloned.1.call-done, bf16[4,128,2048]{2,1,0:T(8,128)(2,1)S(1)} %copy-done), kind=kOutput, calls=%fused_computation.8 | convolution fusion | flops 4294967296 | bytes 14680064 | tf_op jit(solution)/shard_map/dot_general | solution.py:13
  349.2 0.0 copy-start.2
  349.3 7.5 %fusion.4 = f32[4,128,2048,1]{2,1,0,3:T(8,128)S(1)} fusion(bf16[4,512,2048]{2,1,0:T(8,128)(2,1)} %all-gather.2.cloned.1.call-done, f32[4,128,4,512]{3,1,2,0:T(8,128)S(1)} %fusion.8, f32[512]{0:T(512)S(1)} %copy-done.3, f32[4,128,4]{1,0,2:T(4,128)S(1)} %get-tuple-element.6), kind=kOutput, calls=%fused_computation.4 | convolution fusion | flops 4300210176 | bytes 16787456 | tf_op jit(solution)/shard_map/dot_general | solution.py:52
  356.7 9.4 %collective-permute-done.2 = bf16[4,128,2048]{2,1,0:T(8,128)(2,1)S(1)} collective-permute-done((bf16[4,128,2048]{2,1,0:T(8,128)(2,1)S(1)}, bf16[4,128,2048]{2,1,0:T(8,128)(2,1)S(1)}, u32[]{:S(2)}, u32[]{:S(2)}) %collective-permute-start.2) | collective-permute-done | bytes 2097184 | tf_op jit(solution)/shard_map/ppermute | solution.py:9
  366.2 0.0 copy-done.2
  366.2 9.6 %fusion.11 = bf16[4,128,2048]{2,1,0:T(8,128)(2,1)} fusion(f32[4,128,2048,1]{2,1,0,3:T(8,128)S(1)} %fusion.4, bf16[4,128,2048]{2,1,0:T(8,128)(2,1)S(1)} %collective-permute-done.2, bf16[4,128,4,512]{3,1,0,2:T(8,128)(2,1)S(1)} %copy-done.2, bf16[4,512,2048]{2,1,0:T(8,128)(2,1)} %collective-permute-done), kind=kOutput, calls=%fused_computation.12 | convolution fusion | flops 4299161600 | bytes 18874368 | tf_op jit(solution)/shard_map/dot_general | solution.py:52
  (2 shorter events, 0.0 us)
Async XLA Ops:
  6.5 154.4 %all-gather.2.cloned.1.call-start = ((), (), s32[]{:S(2)}) async-start(), calls=%async_computation.1 | async-start | bytes 10485760 | tf_op jit(solution)/shard_map/all_gather | solution.py:65
  160.9 93.1 %collective-permute-start = (bf16[4,512,2048]{2,1,0:T(8,128)(2,1)}, bf16[4,512,2048]{2,1,0:T(8,128)(2,1)}, u32[]{:S(2)}, u32[]{:S(2)}) collective-permute-start(bf16[4,512,2048]{2,1,0:T(8,128)(2,1)} %all-gather.2.cloned.1.call-done), channel_id=1, source_target_pairs={{0,4},{4,8},{8,12},{12,0},{1,5},{5,9},{9,13},{13,1},{2,6},{6,10},{... | collective-permute-start | bytes 25165832 | tf_op jit(solution)/shard_map/ppermute | solution.py:9
  163.1 90.0 %collective-permute-start.1 = (bf16[4]{0:T(256)(128)(2,1)S(1)}, bf16[4]{0:T(256)(128)(2,1)S(1)}, u32[]{:S(2)}, u32[]{:S(2)}) collective-permute-start(bf16[4]{0:T(256)(128)(2,1)S(1)} %convert_element_type.22), channel_id=1, source_target_pairs={{0,4},{4,8},{8,12},{12,0},{1,5},{5,9},{9,13},{13,1},{2,6},{6,10},{... | collective-permute-start | bytes 32 | tf_op jit(solution)/shard_map/ppermute | solution.py:9
  253.9 8.0 %slice-start = ((s8[8388608]{0:T(1024)(128)(4,1)}), s8[4194304]{0:T(1024)(128)(4,1)S(1)}, s32[]{:S(2)}) async-start(s8[8388608]{0:T(1024)(128)(4,1)} %bitcast.75), calls=%async_computation.2 | async-start | bytes 8388608
  254.0 7.9 %slice-start.1 = ((s8[8388608]{0:T(1024)(128)(4,1)}), s8[4194304]{0:T(1024)(128)(4,1)S(1)}, s32[]{:S(2)}) async-start(s8[8388608]{0:T(1024)(128)(4,1)} %bitcast.75), calls=%async_computation.3 | async-start | bytes 8388608
  254.0 7.9 %copy-start.3 = (f32[512]{0:T(512)S(1)}, f32[512]{0:T(512)}, u32[]{:S(2)}) copy-start(f32[512]{0:T(512)} %param.5) | copy-start | bytes 6148
  268.9 1.3 copy-start.1
  331.5 10.8 %copy-start = (bf16[4,128,2048]{2,1,0:T(8,128)(2,1)S(1)}, bf16[4,128,2048]{2,1,0:T(8,128)(2,1)}, u32[]{:S(2)}) copy-start(bf16[4,128,2048]{2,1,0:T(8,128)(2,1)} %param.3) | copy-start | bytes 6291460
  340.2 26.0 %collective-permute-start.2 = (bf16[4,128,2048]{2,1,0:T(8,128)(2,1)S(1)}, bf16[4,128,2048]{2,1,0:T(8,128)(2,1)S(1)}, u32[]{:S(2)}, u32[]{:S(2)}) collective-permute-start(bf16[4,128,2048]{2,1,0:T(8,128)(2,1)S(1)} %convolution_convert_fusion), channel_id=1, source_target_pairs={{0,12},{4,0},{8,4},{12,8},{1,13},{5,1},{9,5},{13,9},{2,14},{6,2},{... | collective-permute-start | bytes 6291464 | tf_op jit(solution)/shard_map/ppermute | solution.py:9
  349.2 16.9 %copy-start.2 = (bf16[4,128,4,512]{3,1,0,2:T(8,128)(2,1)S(1)}, bf16[4,128,4,512]{3,1,0,2:T(8,128)(2,1)}, u32[]{:S(2)}) copy-start(bf16[4,128,4,512]{3,1,0,2:T(8,128)(2,1)} %copy-done.1) | copy-start | bytes 6291460
Sparse Core Ops, SparseCore 0:
  8.9 151.9 all-gather.1
where the time goes:
time: 383 us
  waiting for transfers between devices  253 us (66%)
  blocking collectives  50.8 us (13%)
  matrix products  47.5 us (12%)
  between operations  13.5 us (4%)
  local copies, waits for them, and re-layouts  12.6 us (3%)
    all_gather x1, waiting for transfers between devices, local(): own_full = lax.all_gather(three_index, 'virt', axis=1, tiled=True)  154 us
    ppermute x3, waiting for transfers between devices, shifted(): lax.ppermute(shard, axis, [(i, (i + by) % devices) for i in range(devices)])  98.7 us
    all_to_all x1, blocking collectives, local(): lax.all_to_all(tbar, 'virt', split_axis=3, concat_axis=1, tiled=True)  50.8 us
    dot_general x3, matrix products, contract(): lax.dot_general(left, right, (((1,), (1,)), ((), ())), preferred_element_...  21.7 us
    dot_general x2, matrix products, pair_block(): jnp.dot(flat, part_full.reshape(occ_count * virt_count, aux_count), prefe...  17.1 us
    dot_general x1, matrix products, local(): lax.dot_general(tiles.reshape(occ_count * virt_count, occ_count * rows_he...  8.65 us
  transfers between devices with their start and end apart: 4, of which 3 were waited for; matrix products, arithmetic and copies ran while one was open for 4% of the time, Pallas kernels for 0%

commit v1 on v0

v1 whole, which is shorter than its diff:
```python
import functools

import jax
import jax.numpy as jnp
from jax import lax
from jax.experimental import pallas as pl
from jax.experimental.pallas import tpu as pltpu
from jax.sharding import PartitionSpec as P

LANES = 128
VMEM_BYTES = 48 * 2**20


def shifted(shard, axis, by):
    devices = lax.axis_size(axis)
    return lax.ppermute(shard, axis, [(i, (i + by) % devices) for i in range(devices)])


def contract(left, right):
    return lax.dot_general(
        left, right, (((1,), (1,)), ((), ())), preferred_element_type=jnp.float32
    )


def tile_plain(rows, tile, energies, sums, want):
    own_rows, part_rows = rows
    own_tile, part_tile = tile
    energy_own, energy_part, virt_rows, virt_tile = energies
    occ, here, there = energy_own.shape[0], virt_rows.shape[0], virt_tile.shape[0]
    shape = (occ, there, occ, here)
    diag = contract(own_tile, own_rows).reshape(shape)
    first = contract(part_tile, own_rows).reshape(shape)
    second = contract(own_tile, part_rows).reshape(shape)
    virt = virt_tile[None, :, None, None] + virt_rows[None, None, None, :]
    denom_diag = energy_own[:, None, None, None] + energy_own[None, None, :, None] - virt
    denom_cross = energy_part[:, None, None, None] + energy_own[None, None, :, None] - virt
    swap = (2, 1, 0, 3)
    t_diag = ((2.0 * diag - diag.transpose(swap)) / denom_diag).astype(jnp.bfloat16)
    t_cross = ((2.0 * first - second.transpose(swap)) / denom_cross).astype(jnp.bfloat16)
    t_back = ((2.0 * second - first.transpose(swap)) / denom_cross.transpose(swap)).astype(jnp.bfloat16)

    def spread(amplitudes, rows):
        return lax.dot_general(
            amplitudes.reshape(occ * there, occ * here),
            rows,
            (((0,), (0,)), ((), ())),
            preferred_element_type=jnp.float32,
        )

    terms = {
        "own": lambda: spread(t_diag, own_tile) + spread(t_cross, part_tile),
        "partner": lambda: spread(t_back, own_tile),
    }
    return [terms[name]() if total is None else total + terms[name]() for name, total in zip(want, sums)]


def tile_kernel(
    occ, here, there, columns, want, summed, energy_own, energy_part, virt_rows, virt_tile,
    own_rows, part_rows, own_tile, part_tile, *refs,
):
    sums = refs[:len(want)] if summed else (None,) * len(want)
    refs = refs[len(want):] if summed else refs
    outs = refs[:len(want)]
    tiles, gram, first, second, left, sem = refs[len(want):]
    wide = occ * there
    own, partner = "own" in want, "partner" in want
    step = pl.program_id(0)

    @pl.when(step == 0)
    def _():
        copies = [
            pltpu.make_async_copy(own_tile, tiles.at[pl.ds(0, wide)], sem.at[0]),
            pltpu.make_async_copy(part_tile, tiles.at[pl.ds(wide, wide)], sem.at[1]),
        ]
        for copy in copies:
            copy.start()
        copies[0].wait()
        if own:
            gram[...] = contract(tiles[:wide], own_rows[...])
        second[...] = contract(tiles[:wide], part_rows[...])
        copies[1].wait()
        first[...] = contract(tiles[wide:], own_rows[...])
        virt = virt_tile[...] + virt_rows[...]

        def block(ref, r, c):
            return ref[r * there:(r + 1) * there, c * here:(c + 1) * here]

        def place(column, blocks, c):
            left[c * here:(c + 1) * here, column:column + wide] = (
                jnp.concatenate(blocks, axis=0).T.astype(jnp.bfloat16)
            )

        for i in range(occ):
            if own:
                place(0, [
                    (2.0 * block(gram, j, i) - block(gram, i, j)) / (energy_own[i] + energy_own[j] - virt)
                    for j in range(occ)
                ], i)
                place(wide, [
                    (2.0 * block(first, j, i) - block(second, i, j)) / (energy_own[i] + energy_part[j] - virt)
                    for j in range(occ)
                ], i)
        if partner:
            for j in range(occ):
                place(2 * wide if own else 0, [
                    (2.0 * block(second, i, j) - block(first, j, i)) / (energy_own[i] + energy_part[j] - virt)
                    for i in range(occ)
                ], j)

    at = pl.ds(pl.multiple_of(step * columns, columns), columns)
    for name, total, out in zip(want, sums, outs):
        if name == "own":
            term = jnp.dot(left[:, :2 * wide], tiles[:, at], preferred_element_type=jnp.float32)
        else:
            begin = 2 * wide if own else 0
            term = jnp.dot(
                left[:, begin:begin + wide], tiles[pl.ds(0, wide), at], preferred_element_type=jnp.float32
            )
        out[...] = (term if total is None else total[...] + term).astype(out.dtype)


def tile_terms(rows, tile, energies, sums, want, kinds=None):
    energy_own, energy_part, virt_rows, virt_tile = energies
    occ, here, there = energy_own.shape[0], virt_rows.shape[0], virt_tile.shape[0]
    kinds = kinds or (jnp.float32,) * len(want)
    if here % LANES or (occ * there) % LANES or there % 16:
        return [t.astype(k) for t, k in zip(tile_plain(rows, tile, energies, sums, want), kinds)]
    aux = rows[0].shape[1]
    columns = min(aux, 512)
    wide, tall = occ * there, occ * here
    summed = sums[0] is not None
    scalar = pl.BlockSpec(memory_space=pltpu.SMEM)
    whole = lambda shape: pl.BlockSpec(shape, lambda p: (0, 0))
    column = pl.BlockSpec((tall, columns), lambda p: (0, p))
    hbm = pl.BlockSpec(memory_space=pl.ANY)
    products = 3 if "own" in want else 2
    spreads = (2 if "own" in want else 0) + (1 if "partner" in want else 0)
    return pl.pallas_call(
        functools.partial(tile_kernel, occ, here, there, columns, want, summed),
        grid=(aux // columns,),
        in_specs=[
            scalar, scalar, whole((1, here)), whole((there, 1)),
            whole((tall, aux)), whole((tall, aux)), hbm, hbm,
        ] + ([column] * len(want) if summed else []),
        out_specs=[column] * len(want),
        out_shape=[jax.ShapeDtypeStruct((tall, aux), kind) for kind in kinds],
        scratch_shapes=[
            pltpu.VMEM((2 * wide, aux), jnp.bfloat16),
            pltpu.VMEM((wide, tall), jnp.float32),
            pltpu.VMEM((wide, tall), jnp.float32),
            pltpu.VMEM((wide, tall), jnp.float32),
            pltpu.VMEM((tall, spreads * wide), jnp.bfloat16),
            pltpu.SemaphoreType.DMA((2,)),
        ],
        compiler_params=pltpu.CompilerParams(vmem_limit_bytes=VMEM_BYTES),
        cost_estimate=pl.CostEstimate(
            flops=2 * (products + spreads) * wide * tall * aux,
            bytes_accessed=4 * aux * (tall + wide) + 8 * tall * aux * len(want),
            transcendentals=0,
        ),
    )(
        energy_own, energy_part, virt_rows[None, :], virt_tile[:, None],
        *rows, *tile, *(sums if summed else ()),
    )


def local(three_index, occ_energy, virt_energy):
    occ, here, aux = three_index.shape
    steps = lax.axis_size("virt")
    me = lax.axis_index("virt")
    chunks = 2 if here % 64 == 0 else 1
    size = here // chunks
    energy_part = shifted(occ_energy, "blk", 1)
    virt_rows = lax.dynamic_slice_in_dim(virt_energy, me * here, here, 0)
    own_rows = three_index.reshape(occ * here, aux)
    part_rows = shifted(own_rows, "blk", 1)

    def cut(rows, c):
        return rows.reshape(occ, here, aux)[:, c * size:(c + 1) * size].reshape(occ * size, aux)

    tiles = [cut(own_rows, c) for c in range(chunks)]
    parts = [cut(part_rows, c) for c in range(chunks)]
    rows = (own_rows, part_rows)
    sums = (None, None)
    both = ("own", "partner")
    for step in range(steps):
        later = [shifted(tile, "virt", 1) for tile in tiles] if step < steps - 1 else None
        if step:
            parts = [shifted(tile, "blk", 1) for tile in tiles]
        start = lax.rem(me - step + steps, steps) * here
        for c in range(chunks):
            virt_tile = lax.dynamic_slice_in_dim(virt_energy, start + c * size, size, 0)
            energies = (occ_energy, energy_part, virt_rows, virt_tile)
            tile = (tiles[c], parts[c])
            if step == steps - 1 and c == chunks - 1:
                partner, = tile_terms(rows, tile, energies, sums[1:], ("partner",), (jnp.bfloat16,))
                back = shifted(partner, "blk", -1)
                own, = tile_terms(rows, tile, energies, sums[:1], ("own",))
            else:
                sums = tile_terms(rows, tile, energies, sums, both)
        tiles = later
    return (own + back.astype(jnp.float32)).astype(jnp.bfloat16).reshape(occ, here, aux)


def solution(mesh):
    placed = (P(("copies", "blk"), "virt", None), P(("copies", "blk")), P("copies"))
    return jax.shard_map(
        local,
        mesh=mesh,
        in_specs=placed,
        out_specs=P(("copies", "blk"), "virt", None),
        check_vma=False,
    )
```

time: 383 us -> 229 us (0.60)
  waiting for transfers between devices: 253 us -> 114 us
  Pallas kernels: 0 us -> 93.7 us
  blocking collectives: 50.8 us -> 0 us
  matrix products: 47.5 us -> 0 us
  between operations: 13.5 us -> 0.18 us
  local copies, waits for them, and re-layouts: 12.6 us -> 5.28 us
  starting transfers between devices: 3.7 us -> 10.3 us
    all_gather x1 -> x0, waiting for transfers between devices: 154 us -> none  [local(): own_full = lax.all_gather(three_index, 'virt', axis=1, tiled=True)]
    pallas_call x0 -> x9, Pallas kernels: none -> 93.7 us  [tile_terms(): pl.pallas_call(functools.partial(tile_kernel, occ, here, there, columns,...]
    all_to_all x1 -> x0, blocking collectives: 50.8 us -> none  [local(): lax.all_to_all(tbar, 'virt', split_axis=3, concat_axis=1, tiled=True)]
    dot_general x6 -> x0, matrix products: 47.5 us -> none  [the longest x3 21.7 us: contract(): lax.dot_general(left, right, (((1,), (1,)), ((), ())), preferred_element_...]
    ppermute x3 -> x15, waiting for transfers between devices: 98.7 us -> 114 us  [shifted(): lax.ppermute(shard, axis, [(i, (i + by) % devices) for i in range(devices)])]
    ppermute x3 -> x15, starting transfers between devices: 3.7 us -> 10.3 us  [shifted(): lax.ppermute(shard, axis, [(i, (i + by) % devices) for i in range(devices)])]
  transfers between devices with their start and end apart: 4 -> 15, of which waited for: 3 -> 7; matrix products, arithmetic and copies ran while one was open for 4% -> 2% of each run, Pallas kernels for 0% -> 38%
where the time goes in v1:
time: 229 us; the launch traced here: 228 us
  waiting for transfers between devices  114 us (50%)
  Pallas kernels  93.7 us (41%)
  starting transfers between devices  10.3 us (4%)
  local copies, waits for them, and re-layouts  5.28 us (2%)
  other arithmetic  4.24 us (2%)
    ppermute x15, waiting for transfers between devices, shifted(): lax.ppermute(shard, axis, [(i, (i + by) % devices) for i in range(devices)])  114 us
    pallas_call x9, Pallas kernels, tile_terms(): pl.pallas_call(functools.partial(tile_kernel, occ, here, there, columns,...  93.7 us
    ppermute x15, starting transfers between devices, shifted(): lax.ppermute(shard, axis, [(i, (i + by) % devices) for i in range(devices)])  10.3 us
  transfers between devices with their start and end apart: 15, of which 7 were waited for; matrix products, arithmetic and copies ran while one was open for 2% of the time, Pallas kernels for 38%

profile of v1, /device:TPU:1, one launch (start us, length us, event | category | flops | bytes accessed | tf_op | source)
XLA Modules:
  0.0 228.0 jit_solution(2884685287874522218)
XLA Ops:
  0.0 0.0 copy-start.4
  0.0 0.0 copy-start.5
  0.0 0.0 copy-start
  0.0 2.7 %collective-permute-start.1 = (bf16[512,2048]{1,0:T(8,128)(2,1)}, bf16[512,2048]{1,0:T(8,128)(2,1)}, u32[]{:S(2)}, u32[]{:S(2)}) collective-permute-start(bf16[512,2048]{1,0:T(8,128)(2,1)} %bitcast.25), channel_id=1, source_target_pairs={{0,4},{4,8},{8,12},{12,0},{1,5},{5,9},{9,13},{13,1},{2,6},{6,10},{... | collective-permute-start | bytes 6291464 | tf_op jit(solution)/shard_map/ppermute | solution.py:16
  2.7 1.7 fusion.1
  4.3 1.3 collective-permute-start.6
  5.7 0.0 copy-start.2
  5.7 1.0 copy-done.2
  6.7 1.3 collective-permute-start.2
  8.0 23.5 %collective-permute-done.6.own_tile = bf16[256,2048]{1,0:T(8,128)(2,1)} collective-permute-done((bf16[256,2048]{1,0:T(8,128)(2,1)S(1)}, bf16[256,2048]{1,0:T(8,128)(2,1)}, u32[]{:S(2)}, u32[]{:S(2)}) %collective-permute-start.6) | collective-permute-done | bytes 1048608 | tf_op jit(solution)/shard_map/ppermute | solution.py:16
  31.5 0.0 collective-permute-start.7
  31.5 22.5 %collective-permute-done.2.own_tile = bf16[256,2048]{1,0:T(8,128)(2,1)} collective-permute-done((bf16[256,2048]{1,0:T(8,128)(2,1)S(1)}, bf16[256,2048]{1,0:T(8,128)(2,1)}, u32[]{:S(2)}, u32[]{:S(2)}) %collective-permute-start.2) | collective-permute-done | bytes 1048608 | tf_op jit(solution)/shard_map/ppermute | solution.py:16
  54.0 0.0 collective-permute-start.3
  54.0 0.0 copy-done.4
  54.0 0.9 collective-permute-start
  54.9 0.1 collective-permute-start.13
  55.0 0.0 copy-done.5
  55.0 0.1 dynamic-slice_bitcast_fusion
  55.1 0.1 copy.4.virt_tile
  55.2 0.1 copy.5.virt_tile
  55.3 0.1 copy.6.virt_tile
  55.4 0.1 copy.7.virt_tile
  55.5 0.1 copy.8.virt_tile
  55.6 0.1 copy.9.virt_tile
  55.7 0.1 copy.10.virt_tile
  55.8 0.1 copy.11.virt_tile
  55.9 0.0 copy-start.3
  55.9 0.1 dynamic-slice_bitcast_fusion.8.virt_rows
  55.9 0.0 collective-permute-done.1.part_rows
  55.9 0.0 collective-permute-start.12
  56.0 20.5 %collective-permute-done.7.own_tile = bf16[256,2048]{1,0:T(8,128)(2,1)} collective-permute-done((bf16[256,2048]{1,0:T(8,128)(2,1)}, bf16[256,2048]{1,0:T(8,128)(2,1)}, u32[]{:S(2)}, u32[]{:S(2)}) %collective-permute-start.7) | collective-permute-done | bytes 1048608 | tf_op jit(solution)/shard_map/ppermute | solution.py:16
  76.4 0.0 collective-permute-start.8
  76.4 22.4 %collective-permute-done.3.own_tile = bf16[256,2048]{1,0:T(8,128)(2,1)} collective-permute-done((bf16[256,2048]{1,0:T(8,128)(2,1)}, bf16[256,2048]{1,0:T(8,128)(2,1)}, u32[]{:S(2)}, u32[]{:S(2)}) %collective-permute-start.3) | collective-permute-done | bytes 1048608 | tf_op jit(solution)/shard_map/ppermute | solution.py:16
  98.8 0.0 collective-permute-start.4
  98.8 1.7 fusion
  100.5 0.0 collective-permute-done.energy_part
  100.5 1.1 collective-permute-start.11
  101.6 0.0 copy-done
  101.6 0.0 copy-done.3
  101.6 8.5 %shard_map.37 = (f32[512,2048]{1,0:T(8,128)}, f32[512,2048]{1,0:T(8,128)}) custom-call(f32[4]{0:T(128)S(1)} %copy-done.4, f32[4]{0:T(128)S(1)} %collective-permute-done.energy_part, f32[1,128]{1,0:T(1,128)S(1)} %dynamic-slice_bitcast_fusion.8.virt_rows, f32[64,1]{1,0:T(8,128)S(1)} %copy.4.virt_tile, bf16[512,2048]{1,0:T(8,128)(2,1)S(1)} %bitcast.27, ...), custom_call_target="tpu_custom_call" | custom-call | flops 3221225472 | bytes 23068672 | tf_op jit(solution)/shard_map/pallas_call | solution.py:138
  110.1 0.0 collective-permute-done.13.part_tile
  110.1 0.1 collective-permute-start.10
  110.2 10.7 %shard_map.38 = (f32[512,2048]{1,0:T(8,128)}, f32[512,2048]{1,0:T(8,128)}) custom-call(f32[4]{0:T(128)S(1)} %copy-done.4, f32[4]{0:T(128)S(1)} %collective-permute-done.energy_part, f32[1,128]{1,0:T(1,128)S(1)} %dynamic-slice_bitcast_fusion.8.virt_rows, f32[64,1]{1,0:T(8,128)S(1)} %copy.5.virt_tile, bf16[512,2048]{1,0:T(8,128)(2,1)S(1)} %bitcast.28, ...), custom_call_target="tpu_custom_call" | custom-call | flops 3221225472 | bytes 23068672 | tf_op jit(solution)/shard_map/pallas_call | solution.py:138
  120.9 0.3 collective-permute-done.8.own_tile
  121.3 0.9 collective-permute-start.9
  122.2 12.0 %shard_map.39 = (f32[512,2048]{1,0:T(8,128)}, f32[512,2048]{1,0:T(8,128)}) custom-call(f32[4]{0:T(128)S(1)} %copy-done.4, f32[4]{0:T(128)S(1)} %collective-permute-done.energy_part, f32[1,128]{1,0:T(1,128)S(1)} %dynamic-slice_bitcast_fusion.8.virt_rows, f32[64,1]{1,0:T(8,128)S(1)} %copy.6.virt_tile, bf16[512,2048]{1,0:T(8,128)(2,1)S(1)} %bitcast.29, ...), custom_call_target="tpu_custom_call" | custom-call | flops 3221225472 | bytes 23068672 | tf_op jit(solution)/shard_map/pallas_call | solution.py:138
  134.2 8.5 %collective-permute-done.4.own_tile = bf16[256,2048]{1,0:T(8,128)(2,1)S(1)} collective-permute-done((bf16[256,2048]{1,0:T(8,128)(2,1)}, bf16[256,2048]{1,0:T(8,128)(2,1)S(1)}, u32[]{:S(2)}, u32[]{:S(2)}) %collective-permute-start.4) | collective-permute-done | bytes 1048608 | tf_op jit(solution)/shard_map/ppermute | solution.py:16
  142.7 1.6 collective-permute-start.5
  144.3 0.0 collective-permute-done.12.part_tile
  144.3 12.0 %shard_map.40 = (f32[512,2048]{1,0:T(8,128)}, f32[512,2048]{1,0:T(8,128)}) custom-call(f32[4]{0:T(128)S(1)} %copy-done.4, f32[4]{0:T(128)S(1)} %collective-permute-done.energy_part, f32[1,128]{1,0:T(1,128)S(1)} %dynamic-slice_bitcast_fusion.8.virt_rows, f32[64,1]{1,0:T(8,128)S(1)} %copy.7.virt_tile, bf16[512,2048]{1,0:T(8,128)(2,1)S(1)} %bitcast.30, ...), custom_call_target="tpu_custom_call" | custom-call | flops 3221225472 | bytes 23068672 | tf_op jit(solution)/shard_map/pallas_call | solution.py:138
  156.3 0.0 collective-permute-done.11.part_tile
  156.3 12.0 %shard_map.41 = (f32[512,2048]{1,0:T(8,128)}, f32[512,2048]{1,0:T(8,128)}) custom-call(f32[4]{0:T(128)S(1)} %copy-done.4, f32[4]{0:T(128)S(1)} %collective-permute-done.energy_part, f32[1,128]{1,0:T(1,128)S(1)} %dynamic-slice_bitcast_fusion.8.virt_rows, f32[64,1]{1,0:T(8,128)S(1)} %copy.8.virt_tile, bf16[512,2048]{1,0:T(8,128)(2,1)S(1)} %bitcast.31, ...), custom_call_target="tpu_custom_call" | custom-call | flops 3221225472 | bytes 23068672 | tf_op jit(solution)/shard_map/pallas_call | solution.py:138
  168.4 0.0 collective-permute-done.10.part_tile
  168.4 12.0 %shard_map.42 = (f32[512,2048]{1,0:T(8,128)}, f32[512,2048]{1,0:T(8,128)}) custom-call(f32[4]{0:T(128)S(1)} %copy-done.4, f32[4]{0:T(128)S(1)} %collective-permute-done.energy_part, f32[1,128]{1,0:T(1,128)S(1)} %dynamic-slice_bitcast_fusion.8.virt_rows, f32[64,1]{1,0:T(8,128)S(1)} %copy.9.virt_tile, bf16[512,2048]{1,0:T(8,128)(2,1)S(1)} %bitcast.32, ...), custom_call_target="tpu_custom_call" | custom-call | flops 3221225472 | bytes 23068672 | tf_op jit(solution)/shard_map/pallas_call | solution.py:138
  180.3 0.0 collective-permute-done.9.part_tile
  180.4 10.8 %shard_map.43 = (f32[512,2048]{1,0:T(8,128)}, f32[512,2048]{1,0:T(8,128)}) custom-call(f32[4]{0:T(128)S(1)} %copy-done.4, f32[4]{0:T(128)S(1)} %collective-permute-done.energy_part, f32[1,128]{1,0:T(1,128)S(1)} %dynamic-slice_bitcast_fusion.8.virt_rows, f32[64,1]{1,0:T(8,128)S(1)} %copy.10.virt_tile, bf16[512,2048]{1,0:T(8,128)(2,1)S(1)} %bitcast.33, ...), custom_call_target="tpu_custom_call" | custom-call | flops 3221225472 | bytes 23068672 | tf_op jit(solution)/shard_map/pallas_call | solution.py:138
  191.2 0.0 collective-permute-done.5.part_tile
  191.2 0.0 copy-start.1
  191.2 6.9 %shard_map.45 = bf16[512,2048]{1,0:T(8,128)(2,1)S(1)} custom-call(f32[4]{0:T(128)S(1)} %copy-done.4, f32[4]{0:T(128)S(1)} %collective-permute-done.energy_part, f32[1,128]{1,0:T(1,128)S(1)} %dynamic-slice_bitcast_fusion.8.virt_rows, f32[64,1]{1,0:T(8,128)S(1)} %copy.11.virt_tile, bf16[512,2048]{1,0:T(8,128)(2,1)} %bitcast.26, ...), custom_call_target="tpu_custom_call" | custom-call | flops 1610612736 | bytes 14680064 | tf_op jit(solution)/shard_map/pallas_call | solution.py:138
  198.1 0.3 collective-permute-start.14
  198.4 0.0 copy-done.1
  198.4 8.8 %shard_map.44 = f32[512,2048]{1,0:T(8,128)} custom-call(f32[4]{0:T(128)S(1)} %copy-done.4, f32[4]{0:T(128)S(1)} %collective-permute-done.energy_part, f32[1,128]{1,0:T(1,128)S(1)} %dynamic-slice_bitcast_fusion.8.virt_rows, f32[64,1]{1,0:T(8,128)S(1)} %copy.11.virt_tile, bf16[512,2048]{1,0:T(8,128)(2,1)S(1)} %bitcast.34, ...), custom_call_target="tpu_custom_call" | custom-call | flops 2684354560 | bytes 14680064 | tf_op jit(solution)/shard_map/pallas_call | solution.py:138
  207.2 16.6 %collective-permute-done.14 = bf16[512,2048]{1,0:T(8,128)(2,1)S(1)} collective-permute-done((bf16[512,2048]{1,0:T(8,128)(2,1)S(1)}, bf16[512,2048]{1,0:T(8,128)(2,1)S(1)}, u32[]{:S(2)}, u32[]{:S(2)}) %collective-permute-start.14) | collective-permute-done | bytes 2097184 | tf_op jit(solution)/shard_map/ppermute | solution.py:16
  223.8 4.2 %add_convert_fusion = bf16[512,2048]{1,0:T(8,128)(2,1)} fusion(f32[512,2048]{1,0:T(8,128)} %shard_map.44, bf16[512,2048]{1,0:T(8,128)(2,1)S(1)} %collective-permute-done.14), kind=kLoop, calls=%fused_computation | loop fusion | flops 3145728 | bytes 8388608 | tf_op jit(solution)/shard_map/convert_element_type | solution.py:202
Async XLA Ops:
  0.0 54.0 %copy-start.4 = (f32[4]{0:T(128)S(1)}, f32[4]{0:T(128)}, u32[]{:S(2)}) copy-start(f32[4]{0:T(128)} %energy_own.17) | copy-start | bytes 52
  0.0 55.0 %copy-start.5 = (f32[512]{0:T(512)S(1)}, f32[512]{0:T(512)}, u32[]{:S(2)}) copy-start(f32[512]{0:T(512)} %param.5) | copy-start | bytes 6148
  0.0 101.6 %copy-start = (bf16[4,128,2048]{2,1,0:T(8,128)(2,1)S(1)}, bf16[4,128,2048]{2,1,0:T(8,128)(2,1)}, u32[]{:S(2)}) copy-start(bf16[4,128,2048]{2,1,0:T(8,128)(2,1)} %param.3) | copy-start | bytes 6291460
  0.0 55.9 %collective-permute-start.1 = (bf16[512,2048]{1,0:T(8,128)(2,1)}, bf16[512,2048]{1,0:T(8,128)(2,1)}, u32[]{:S(2)}, u32[]{:S(2)}) collective-permute-start(bf16[512,2048]{1,0:T(8,128)(2,1)} %bitcast.25), channel_id=1, source_target_pairs={{0,4},{4,8},{8,12},{12,0},{1,5},{5,9},{9,13},{13,1},{2,6},{6,10},{... | collective-permute-start | bytes 6291464 | tf_op jit(solution)/shard_map/ppermute | solution.py:16
  4.3 27.2 %collective-permute-start.6 = (bf16[256,2048]{1,0:T(8,128)(2,1)S(1)}, bf16[256,2048]{1,0:T(8,128)(2,1)}, u32[]{:S(2)}, u32[]{:S(2)}) collective-permute-start(bf16[256,2048]{1,0:T(8,128)(2,1)S(1)} %bitcast.38), channel_id=1, source_target_pairs={{0,1},{1,2},{2,3},{3,0},{4,5},{5,6},{6,7},{7,4},{8,9},{9,10},{10,1... | collective-permute-start | bytes 3145736 | tf_op jit(solution)/shard_map/ppermute | solution.py:16
  5.7 1.0 copy-start.2
  6.7 47.3 %collective-permute-start.2 = (bf16[256,2048]{1,0:T(8,128)(2,1)S(1)}, bf16[256,2048]{1,0:T(8,128)(2,1)}, u32[]{:S(2)}, u32[]{:S(2)}) collective-permute-start(bf16[256,2048]{1,0:T(8,128)(2,1)S(1)} %bitcast.35), channel_id=1, source_target_pairs={{0,1},{1,2},{2,3},{3,0},{4,5},{5,6},{6,7},{7,4},{8,9},{9,10},{10,1... | collective-permute-start | bytes 3145736 | tf_op jit(solution)/shard_map/ppermute | solution.py:16
  31.5 44.9 %collective-permute-start.7 = (bf16[256,2048]{1,0:T(8,128)(2,1)}, bf16[256,2048]{1,0:T(8,128)(2,1)}, u32[]{:S(2)}, u32[]{:S(2)}) collective-permute-start(bf16[256,2048]{1,0:T(8,128)(2,1)} %collective-permute-done.6.own_tile), channel_id=1, source_target_pairs={{0,1},{1,2},{2,3},{3,0},{4,5},{5,6},{6,7},{7,4},{8,9},{9,10},{10,1... | collective-permute-start | bytes 3145736 | tf_op jit(solution)/shard_map/ppermute | solution.py:16
  54.0 44.8 %collective-permute-start.3 = (bf16[256,2048]{1,0:T(8,128)(2,1)}, bf16[256,2048]{1,0:T(8,128)(2,1)}, u32[]{:S(2)}, u32[]{:S(2)}) collective-permute-start(bf16[256,2048]{1,0:T(8,128)(2,1)} %collective-permute-done.2.own_tile), channel_id=1, source_target_pairs={{0,1},{1,2},{2,3},{3,0},{4,5},{5,6},{6,7},{7,4},{8,9},{9,10},{10,1... | collective-permute-start | bytes 3145736 | tf_op jit(solution)/shard_map/ppermute | solution.py:16
  54.0 46.5 %collective-permute-start = (f32[4]{0:T(128)S(1)}, f32[4]{0:T(128)S(1)}, u32[]{:S(2)}, u32[]{:S(2)}) collective-permute-start(f32[4]{0:T(128)S(1)} %copy-done.4), channel_id=1, source_target_pairs={{0,4},{4,8},{8,12},{12,0},{1,5},{5,9},{9,13},{13,1},{2,6},{6,10},{... | collective-permute-start | bytes 56 | tf_op jit(solution)/shard_map/ppermute | solution.py:16
  54.9 55.2 %collective-permute-start.13 = (bf16[256,2048]{1,0:T(8,128)(2,1)}, bf16[256,2048]{1,0:T(8,128)(2,1)}, u32[]{:S(2)}, u32[]{:S(2)}) collective-permute-start(bf16[256,2048]{1,0:T(8,128)(2,1)} %collective-permute-done.6.own_tile), channel_id=1, source_target_pairs={{0,4},{4,8},{8,12},{12,0},{1,5},{5,9},{9,13},{13,1},{2,6},{6,10},{... | collective-permute-start | bytes 3145736 | tf_op jit(solution)/shard_map/ppermute | solution.py:16
  55.9 45.7 %copy-start.3 = (bf16[4,64,2048]{2,1,0:T(8,128)(2,1)S(1)}, bf16[4,64,2048]{2,1,0:T(8,128)(2,1)}, u32[]{:S(2)}) copy-start(bf16[4,64,2048]{2,1,0:T(8,128)(2,1)} %copy-done.2) | copy-start | bytes 3145732
  55.9 88.4 %collective-permute-start.12 = (bf16[256,2048]{1,0:T(8,128)(2,1)}, bf16[256,2048]{1,0:T(8,128)(2,1)S(1)}, u32[]{:S(2)}, u32[]{:S(2)}) collective-permute-start(bf16[256,2048]{1,0:T(8,128)(2,1)} %collective-permute-done.2.own_tile), channel_id=1, source_target_pairs={{0,4},{4,8},{8,12},{12,0},{1,5},{5,9},{9,13},{13,1},{2,6},{6,10},{... | collective-permute-start | bytes 3145736 | tf_op jit(solution)/shard_map/ppermute | solution.py:16
  76.4 44.8 %collective-permute-start.8 = (bf16[256,2048]{1,0:T(8,128)(2,1)}, bf16[256,2048]{1,0:T(8,128)(2,1)S(1)}, u32[]{:S(2)}, u32[]{:S(2)}) collective-permute-start(bf16[256,2048]{1,0:T(8,128)(2,1)} %collective-permute-done.7.own_tile), channel_id=1, source_target_pairs={{0,1},{1,2},{2,3},{3,0},{4,5},{5,6},{6,7},{7,4},{8,9},{9,10},{10,1... | collective-permute-start | bytes 3145736 | tf_op jit(solution)/shard_map/ppermute | solution.py:16
  98.8 43.9 %collective-permute-start.4 = (bf16[256,2048]{1,0:T(8,128)(2,1)}, bf16[256,2048]{1,0:T(8,128)(2,1)S(1)}, u32[]{:S(2)}, u32[]{:S(2)}) collective-permute-start(bf16[256,2048]{1,0:T(8,128)(2,1)} %collective-permute-done.3.own_tile), channel_id=1, source_target_pairs={{0,1},{1,2},{2,3},{3,0},{4,5},{5,6},{6,7},{7,4},{8,9},{9,10},{10,1... | collective-permute-start | bytes 3145736 | tf_op jit(solution)/shard_map/ppermute | solution.py:16
  100.5 55.8 %collective-permute-start.11 = (bf16[256,2048]{1,0:T(8,128)(2,1)}, bf16[256,2048]{1,0:T(8,128)(2,1)S(1)}, u32[]{:S(2)}, u32[]{:S(2)}) collective-permute-start(bf16[256,2048]{1,0:T(8,128)(2,1)} %collective-permute-done.7.own_tile), channel_id=1, source_target_pairs={{0,4},{4,8},{8,12},{12,0},{1,5},{5,9},{9,13},{13,1},{2,6},{6,10},{... | collective-permute-start | bytes 3145736 | tf_op jit(solution)/shard_map/ppermute | solution.py:16
  110.1 58.2 %collective-permute-start.10 = (bf16[256,2048]{1,0:T(8,128)(2,1)}, bf16[256,2048]{1,0:T(8,128)(2,1)S(1)}, u32[]{:S(2)}, u32[]{:S(2)}) collective-permute-start(bf16[256,2048]{1,0:T(8,128)(2,1)} %collective-permute-done.3.own_tile), channel_id=1, source_target_pairs={{0,4},{4,8},{8,12},{12,0},{1,5},{5,9},{9,13},{13,1},{2,6},{6,10},{... | collective-permute-start | bytes 3145736 | tf_op jit(solution)/shard_map/ppermute | solution.py:16
  121.3 59.1 %collective-permute-start.9 = (bf16[256,2048]{1,0:T(8,128)(2,1)S(1)}, bf16[256,2048]{1,0:T(8,128)(2,1)S(1)}, u32[]{:S(2)}, u32[]{:S(2)}) collective-permute-start(bf16[256,2048]{1,0:T(8,128)(2,1)S(1)} %collective-permute-done.8.own_tile), channel_id=1, source_target_pairs={{0,4},{4,8},{8,12},{12,0},{1,5},{5,9},{9,13},{13,1},{2,6},{6,10},{... | collective-permute-start | bytes 3145736 | tf_op jit(solution)/shard_map/ppermute | solution.py:16
  142.7 48.4 %collective-permute-start.5 = (bf16[256,2048]{1,0:T(8,128)(2,1)S(1)}, bf16[256,2048]{1,0:T(8,128)(2,1)S(1)}, u32[]{:S(2)}, u32[]{:S(2)}) collective-permute-start(bf16[256,2048]{1,0:T(8,128)(2,1)S(1)} %collective-permute-done.4.own_tile), channel_id=1, source_target_pairs={{0,4},{4,8},{8,12},{12,0},{1,5},{5,9},{9,13},{13,1},{2,6},{6,10},{... | collective-permute-start | bytes 3145736 | tf_op jit(solution)/shard_map/ppermute | solution.py:16
  191.2 7.2 %copy-start.1 = (bf16[4,128,2048]{2,1,0:T(8,128)(2,1)S(1)}, bf16[4,128,2048]{2,1,0:T(8,128)(2,1)}, u32[]{:S(2)}) copy-start(bf16[4,128,2048]{2,1,0:T(8,128)(2,1)} %param.3) | copy-start | bytes 6291460
  198.1 25.7 %collective-permute-start.14 = (bf16[512,2048]{1,0:T(8,128)(2,1)S(1)}, bf16[512,2048]{1,0:T(8,128)(2,1)S(1)}, u32[]{:S(2)}, u32[]{:S(2)}) collective-permute-start(bf16[512,2048]{1,0:T(8,128)(2,1)S(1)} %shard_map.45), channel_id=1, source_target_pairs={{0,12},{4,0},{8,4},{12,8},{1,13},{5,1},{9,5},{13,9},{2,14},{6,2},{... | collective-permute-start | bytes 6291464 | tf_op jit(solution)/shard_map/ppermute | solution.py:16

commit v2 on v1

v2 whole, which is shorter than its diff:
```python
import functools

import jax
import jax.numpy as jnp
from jax import lax
from jax.experimental import pallas as pl
from jax.experimental.pallas import tpu as pltpu
from jax.sharding import PartitionSpec as P

LANES = 128
VMEM_BYTES = 32 * 2**20


def shifted(shard, axis, by):
    devices = lax.axis_size(axis)
    return lax.ppermute(shard, axis, [(i, (i + by) % devices) for i in range(devices)])


def around(shard, odd):
    groups, devices = lax.axis_size("blk"), lax.axis_size("virt")
    return lax.ppermute(shard, ("blk", "virt"), [
        (g * devices + i, g * devices + (i + 1) % devices)
        for g in range(odd, groups, 2)
        for i in range(devices)
    ])


def passed(shard, odd, by):
    groups = lax.axis_size("blk")
    return lax.ppermute(shard, "blk", [(g, (g + by) % groups) for g in range(odd, groups, 2)])


def in_odd_group():
    return lax.rem(lax.axis_index("blk"), 2) == 1


def contract(left, right):
    return lax.dot_general(
        left, right, (((1,), (1,)), ((), ())), preferred_element_type=jnp.float32
    )


def first_row(span, here):
    step, begin = span
    steps = lax.axis_size("virt")
    return lax.rem(lax.axis_index("virt") + (steps - step), steps) * here + begin


def tile_plain(rows, tile, energies, sums, want, span):
    own_rows, part_rows = rows
    own_tile, part_tile = tile
    energy_own, energy_part, virt_rows, virt_column = energies
    occ, here = energy_own.shape[0], virt_rows.shape[1]
    there = own_tile.shape[0] // occ
    virt_rows = virt_rows[0]
    virt_tile = lax.dynamic_slice_in_dim(virt_column[:, 0], first_row(span, here), there, 0)
    shape = (occ, there, occ, here)
    diag = contract(own_tile, own_rows).reshape(shape)
    first = contract(part_tile, own_rows).reshape(shape)
    second = contract(own_tile, part_rows).reshape(shape)
    virt = virt_tile[None, :, None, None] + virt_rows[None, None, None, :]
    denom_diag = energy_own[:, None, None, None] + energy_own[None, None, :, None] - virt
    denom_cross = energy_part[:, None, None, None] + energy_own[None, None, :, None] - virt
    swap = (2, 1, 0, 3)
    t_diag = ((2.0 * diag - diag.transpose(swap)) / denom_diag).astype(jnp.bfloat16)
    t_cross = ((2.0 * first - second.transpose(swap)) / denom_cross).astype(jnp.bfloat16)
    t_back = ((2.0 * second - first.transpose(swap)) / denom_cross.transpose(swap)).astype(jnp.bfloat16)

    def spread(amplitudes, rows):
        return lax.dot_general(
            amplitudes.reshape(occ * there, occ * here),
            rows,
            (((0,), (0,)), ((), ())),
            preferred_element_type=jnp.float32,
        )

    terms = {
        "own": lambda: spread(t_diag, own_tile) + spread(t_cross, part_tile),
        "partner": lambda: spread(t_back, own_tile),
    }
    return [terms[name]() if total is None else total + terms[name]() for name, total in zip(want, sums)]


def tile_kernel(
    occ, here, sizes, choices, columns, want, summed, span, energy_own, energy_part, virt_rows, virt_column,
    after, own_rows, part_rows, *refs,
):
    del after
    refs = list(refs)
    own_pieces, part_pieces = [[[refs.pop(0) for _ in range(n)] for n in side] for side in choices]
    sums = refs[:len(want)] if summed else (None,) * len(want)
    refs = refs[len(want):] if summed else refs
    outs = refs[:len(want)]
    done, tiles, gram, first, second, left, sem = refs[len(want):]
    done[...] = jnp.zeros_like(done)
    there = sum(sizes)
    wide = occ * there
    own, partner = "own" in want, "partner" in want
    groups = []
    for which, pieces in enumerate((own_pieces, part_pieces)):
        group, offset = [], 0
        for n, (piece, size) in enumerate(zip(pieces, sizes)):
            for j in range(occ):
                group.append([
                    pltpu.make_async_copy(
                        choice.at[pl.ds(j * size, size)],
                        tiles.at[pl.ds(which * wide + j * there + offset, size)],
                        sem.at[(which * len(sizes) + n) * occ + j],
                    )
                    for choice in piece
                ])
            offset += size
        groups.append(group)
    for copies in groups[0] + groups[1]:
        if len(copies) == 1:
            copies[0].start()
        else:
            pl.when(in_odd_group())(copies[1].start)
            pl.when(jnp.logical_not(in_odd_group()))(copies[0].start)
    for copies in groups[0]:
        copies[0].wait()
    if own:
        gram[...] = contract(tiles[:wide], own_rows[...])
    second[...] = contract(tiles[:wide], part_rows[...])
    for copies in groups[1]:
        copies[0].wait()
    first[...] = contract(tiles[wide:], own_rows[...])
    begin = pl.multiple_of(first_row(span, here), 16)
    virt = virt_column[pl.ds(begin, there)] + virt_rows[...]

    def block(ref, r, c):
        return ref[r * there:(r + 1) * there, c * here:(c + 1) * here]

    def place(column, blocks, c):
        left[c * here:(c + 1) * here, column:column + wide] = (
            jnp.concatenate(blocks, axis=0).T.astype(jnp.bfloat16)
        )

    for i in range(occ):
        if own:
            place(0, [
                (2.0 * block(gram, j, i) - block(gram, i, j)) / (energy_own[i] + energy_own[j] - virt)
                for j in range(occ)
            ], i)
            place(wide, [
                (2.0 * block(first, j, i) - block(second, i, j)) / (energy_own[i] + energy_part[j] - virt)
                for j in range(occ)
            ], i)
    if partner:
        for j in range(occ):
            place(2 * wide if own else 0, [
                (2.0 * block(second, i, j) - block(first, j, i)) / (energy_own[i] + energy_part[j] - virt)
                for i in range(occ)
            ], j)

    for begin in range(0, tiles.shape[1], columns):
        at = slice(begin, begin + columns)
        for name, total, out in zip(want, sums, outs):
            if name == "own":
                term = jnp.dot(left[:, :2 * wide], tiles[:, at], preferred_element_type=jnp.float32)
            else:
                skip = 2 * wide if own else 0
                term = jnp.dot(
                    left[:, skip:skip + wide], tiles[:wide, at], preferred_element_type=jnp.float32
                )
            out[:, at] = (term if total is None else total[:, at] + term).astype(out.dtype)


def tile_terms(rows, pieces, energies, sums, want, span, after, kinds=None):
    energy_own, virt_rows = energies[0], energies[2]
    occ, here = energy_own.shape[0], virt_rows.shape[1]
    aux = rows[0].shape[1]
    pieces = [[p if isinstance(p, tuple) else (p,) for p in side] for side in pieces]
    choices = [[len(p) for p in side] for side in pieces]
    sizes = tuple(p[0].shape[0] // occ for p in pieces[0])
    there = sum(sizes)
    kinds = kinds or (jnp.float32,) * len(want)
    if here % LANES or (occ * there) % LANES or any(size % 16 for size in sizes):
        chosen = [[p[0] if len(p) == 1 else jnp.where(in_odd_group(), p[1], p[0]) for p in side] for side in pieces]
        tile = [
            jnp.concatenate([p.reshape(occ, -1, aux) for p in side], axis=1).reshape(occ * there, aux)
            for side in chosen
        ]
        sums = [t.astype(k) for t, k in zip(tile_plain(rows, tile, energies, sums, want, span), kinds)]
        return *sums, sums[0][:1, :1]
    flat_pieces = [p for side in pieces for choice in side for p in choice]
    columns = min(aux, 512)
    wide, tall = occ * there, occ * here
    summed = sums[0] is not None
    scalar = pl.BlockSpec(memory_space=pltpu.SMEM)
    vmem = pl.BlockSpec(memory_space=pltpu.VMEM)
    hbm = pl.BlockSpec(memory_space=pl.ANY)
    products = 3 if "own" in want else 2
    spreads = (2 if "own" in want else 0) + (1 if "partner" in want else 0)
    return pl.pallas_call(
        functools.partial(tile_kernel, occ, here, sizes, choices, columns, want, summed, span),
        in_specs=[scalar, scalar, vmem, vmem, hbm, vmem, vmem] + [hbm] * len(flat_pieces) + [vmem] * (len(want) * summed),
        out_specs=[vmem] * (len(want) + 1),
        out_shape=[
            pltpu.VMEM((tall, aux), kind) if kind == jnp.float32 else jax.ShapeDtypeStruct((tall, aux), kind)
            for kind in kinds
        ] + [jax.ShapeDtypeStruct((8, LANES), jnp.float32)],
        input_output_aliases={
            7 + len(flat_pieces) + n: n for n, kind in enumerate(kinds) if summed and kind == jnp.float32
        },
        scratch_shapes=[
            pltpu.VMEM((2 * wide, aux), jnp.bfloat16),
            pltpu.VMEM((wide, tall), jnp.float32),
            pltpu.VMEM((wide, tall), jnp.float32),
            pltpu.VMEM((wide, tall), jnp.float32),
            pltpu.VMEM((tall, spreads * wide), jnp.bfloat16),
            pltpu.SemaphoreType.DMA((2 * len(sizes) * occ,)),
        ],
        compiler_params=pltpu.CompilerParams(vmem_limit_bytes=VMEM_BYTES),
        cost_estimate=pl.CostEstimate(flops=0, bytes_accessed=0, transcendentals=0),
    )(
        *energies, after, *rows, *flat_pieces, *(sums if summed else ()),
    )


def local(three_index, occ_energy, virt_energy):
    occ, here, aux = three_index.shape
    steps = lax.axis_size("virt")
    me = lax.axis_index("virt")
    sizes = (here // 2,) * 2 if here % LANES == 0 else (here,)
    offsets = [sum(sizes[:c]) for c in range(len(sizes))]
    cut = len(sizes) // 2
    energy_part = shifted(occ_energy, "blk", 1)
    virt_rows = lax.dynamic_slice_in_dim(virt_energy, me * here, here, 0)
    own_rows = three_index.reshape(occ * here, aux)
    part_rows = shifted(own_rows, "blk", 1)
    rows = (own_rows, part_rows)
    both = ("own", "partner")

    energies = (occ_energy, energy_part, virt_rows[None, :], virt_energy[:, None])
    done = jnp.zeros((1, 1), jnp.float32)

    def terms(step, pieces, sums, want, begin, after, kinds=None):
        after, _ = lax.optimization_barrier((done, after))
        *sums, end = tile_terms(rows, pieces, energies, sums, want, (step, begin), after, kinds)
        return sums, end

    tiles = lax.optimization_barrier([
        three_index[:, o:o + size].reshape(occ * size, aux) for o, size in zip(offsets, sizes)
    ])
    ordered = lax.axis_size("blk") % 2 == 0 and cut > 0 and steps > 2
    moving = [shifted(tile, "virt", 1) for tile in tiles]
    waiting = ([own_rows], [part_rows])
    sums = (None, None)
    for step in range(1, steps - ordered):
        tiles, later, parts = [], [], []
        for c, tile in enumerate(moving):
            tile, *_ = lax.optimization_barrier((tile, done, *(parts or waiting[1])[-1:]))
            tiles.append(tile)
            if step < steps - 1 - ordered:
                later.append(shifted(tile, "virt", 1))
            elif ordered:
                later.append(around(tile, 1))
            parts.append(shifted(tile, "blk", 1))
            if c == 0:
                sums, done = terms(step - 1, waiting, sums, both, 0, tile)
        waiting, moving = (tiles, parts), later
    step = steps - 1
    if ordered:
        crossed, behind = [], []
        for c, tile in enumerate(moving):
            tile, *_ = lax.optimization_barrier((tile, done, (crossed or parts)[-1]))
            moving[c] = tile
            crossed.append(passed(tile, 1, 1))
            if c == 0:
                sums, done = terms(step - 1, waiting, sums, both, 0, tile)
            held = tiles[c]
            if c:
                held, _ = lax.optimization_barrier((held, crossed[c - 1]))
            behind.append(around(held, 0))
        tiles, parts = [], []
        for c, tile in enumerate(behind):
            tile, _ = lax.optimization_barrier((tile, done))
            tiles.append((tile, moving[c]))
            parts.append((crossed[c], passed(tile, 0, 1)))
            if c + 1 == cut:
                sums, done = terms(step, (tiles[:cut], parts[:cut]), sums, both, 0, tile)
    begin = offsets[cut]
    tail = (tiles[cut:], parts[cut:])
    (partner,), done = terms(step, tail, sums[1:], ("partner",), begin, done, (jnp.bfloat16,))
    back = shifted(partner, "blk", -1)
    (own,), done = terms(step, tail, sums[:1], ("own",), begin, done)
    return (own + back.astype(jnp.float32)).astype(jnp.bfloat16).reshape(occ, here, aux)


def solution(mesh):
    placed = (P(("copies", "blk"), "virt", None), P(("copies", "blk")), P("copies"))
    return jax.shard_map(
        local,
        mesh=mesh,
        in_specs=placed,
        out_specs=P(("copies", "blk"), "virt", None),
        check_vma=False,
    )
```

time: 229 us -> 184 us (0.80)
  Pallas kernels: 93.7 us -> 39.2 us
  starting transfers between devices: 10.3 us -> 24.9 us
  waiting for transfers between devices: 114 us -> 111 us
    pallas_call x9 -> x6, Pallas kernels: 93.7 us -> 39.2 us  [tile_terms(): pl.pallas_call(functools.partial(tile_kernel, occ, here, sizes, choices,...]
    ppermute x15 -> x11, waiting for transfers between devices: 114 us -> 84.5 us  [shifted(): lax.ppermute(shard, axis, [(i, (i + by) % devices) for i in range(devices)])]
    ppermute x0 -> x8, waiting for transfers between devices: none -> 26.7 us  [the longest x4 17 us: around(): lax.ppermute(shard, ('blk', 'virt'), [(g * devices + i, g * devices + (i...]
    ppermute x0 -> x8, starting transfers between devices: none -> 13.1 us  [the longest x4 7.07 us: passed(): lax.ppermute(shard, 'blk', [(g, (g + by) % groups) for g in range(odd, gr...]
    ppermute x15 -> x11, starting transfers between devices: 10.3 us -> 11.8 us  [shifted(): lax.ppermute(shard, axis, [(i, (i + by) % devices) for i in range(devices)])]
  transfers between devices with their start and end apart: 15 -> 19, of which waited for: 7 -> 9; matrix products, arithmetic and copies ran while one was open for 2% -> 2% of each run, Pallas kernels for 38% -> 20%
where the time goes in v2:
time: 184 us; the launch traced here: 183 us
  waiting for transfers between devices  111 us (60%)
  Pallas kernels  39.2 us (21%)
  starting transfers between devices  24.9 us (14%)
  local copies, waits for them, and re-layouts  5.86 us (3%)
  other arithmetic  2.04 us (1%)
    ppermute x11, waiting for transfers between devices, shifted(): lax.ppermute(shard, axis, [(i, (i + by) % devices) for i in range(devices)])  84.5 us
    pallas_call x6, Pallas kernels, tile_terms(): pl.pallas_call(functools.partial(tile_kernel, occ, here, sizes, choices,...  39.2 us
    ppermute x4, waiting for transfers between devices, around(): lax.ppermute(shard, ('blk', 'virt'), [(g * devices + i, g * devices + (i...  17 us
    ppermute x11, starting transfers between devices, shifted(): lax.ppermute(shard, axis, [(i, (i + by) % devices) for i in range(devices)])  11.8 us
    ppermute x4, waiting for transfers between devices, passed(): lax.ppermute(shard, 'blk', [(g, (g + by) % groups) for g in range(odd, gr...  9.78 us
    ppermute x4, starting transfers between devices, passed(): lax.ppermute(shard, 'blk', [(g, (g + by) % groups) for g in range(odd, gr...  7.07 us
    ppermute x4, starting transfers between devices, around(): lax.ppermute(shard, ('blk', 'virt'), [(g * devices + i, g * devices + (i...  6.03 us
  transfers between devices with their start and end apart: 19, of which 9 were waited for; matrix products, arithmetic and copies ran while one was open for 2% of the time, Pallas kernels for 20%

profile of v2, /device:TPU:1, one launch (start us, length us, event | category | flops | bytes accessed | tf_op | source)
XLA Modules:
  0.0 183.4 jit_solution(5108882009243980025)
XLA Ops:
  0.0 0.0 copy-start
  0.0 0.0 copy-start.4
  0.0 0.0 copy-start.5
  0.0 2.7 %collective-permute-start.2 = (bf16[512,2048]{1,0:T(8,128)(2,1)}, bf16[512,2048]{1,0:T(8,128)(2,1)S(1)}, u32[]{:S(2)}, u32[]{:S(2)}) collective-permute-start(bf16[512,2048]{1,0:T(8,128)(2,1)} %bitcast.7), channel_id=1, source_target_pairs={{0,4},{4,8},{8,12},{12,0},{1,5},{5,9},{9,13},{13,1},{2,6},{6,10},{... | collective-permute-start | bytes 6291464 | tf_op jit(solution)/shard_map/ppermute | solution.py:16
  2.7 2.7 %fusion = (bf16[4,64,2048]{2,1,0:T(8,128)(2,1)}, bf16[4,64,2048]{2,1,0:T(8,128)(2,1)S(1)}) fusion(bf16[4,128,2048]{2,1,0:T(8,128)(2,1)} %param.3), kind=kLoop, calls=%fused_computation.2 | loop fusion | bytes 4194304 | tf_op jit(solution)/shard_map/slice | solution.py:244
  5.4 1.3 collective-permute-start.1
  6.7 1.3 collective-permute-start.4
  8.0 24.4 %collective-permute-done.1.refs_0_ = bf16[256,2048]{1,0:T(8,128)(2,1)} collective-permute-done((bf16[256,2048]{1,0:T(8,128)(2,1)S(1)}, bf16[256,2048]{1,0:T(8,128)(2,1)}, u32[]{:S(2)}, u32[]{:S(2)}) %collective-permute-start.1) | collective-permute-done | bytes 1048608 | tf_op jit(solution)/shard_map/ppermute | solution.py:16
  32.4 0.0 collective-permute-done.2.part_rows.refs_1_
  32.4 0.0 copy-start.1
  32.4 1.3 copy-done.1
  33.7 1.0 collective-permute-start.5
  34.7 0.0 copy-done.4
  34.7 0.0 collective-permute-start
  34.7 0.0 copy-done.5
  34.7 0.1 copy.16.virt_column
  34.9 0.1 dynamic-slice_bitcast_fusion.virt_rows
  35.0 0.0 collective-permute-start.3
  35.0 11.8 %collective-permute-done.energy_part = f32[4]{0:T(128)S(1)} collective-permute-done((f32[4]{0:T(128)S(1)}, f32[4]{0:T(128)S(1)}, u32[]{:S(2)}, u32[]{:S(2)}) %collective-permute-start) | collective-permute-done | bytes 48 | tf_op jit(solution)/shard_map/ppermute | solution.py:16
  46.8 0.0 copy-done
  46.8 0.0 copy-start.2
  46.8 1.6 copy-done.2
  48.4 0.0 copy-start.3
  48.4 8.1 %shard_map.37 = (f32[512,2048]{1,0:T(8,128)S(1)}, f32[512,2048]{1,0:T(8,128)S(1)}, f32[8,128]{1,0:T(8,128)S(1)}) custom-call(f32[4]{0:T(128)S(1)} %copy-done.4, f32[4]{0:T(128)S(1)} %collective-permute-done.energy_part, f32[1,128]{1,0:T(1,128)S(1)} %dynamic-slice_bitcast_fusion.virt_rows, f32[512,1]{1,0:T(8,128)S(1)} %copy.16.virt_column, ...), custom_call_target="tpu_custom_call" | custom-call | tf_op jit(solution)/shard_map/pallas_call | solution.py:195
  56.5 0.0 collective-permute-done.4.refs_1_
  56.5 0.0 collective-permute-done.5.refs_2_
  56.5 2.5 %collective-permute-start.6 = (bf16[256,2048]{1,0:T(8,128)(2,1)S(1)}, bf16[256,2048]{1,0:T(8,128)(2,1)S(1)}, u32[]{:S(2)}, u32[]{:S(2)}) collective-permute-start(bf16[256,2048]{1,0:T(8,128)(2,1)S(1)} %collective-permute-done.4.refs_1_), channel_id=1, source_target_pairs={{0,4},{4,8},{8,12},{12,0},{1,5},{5,9},{9,13},{13,1},{2,6},{6,10},{... | collective-permute-start | bytes 3145736 | tf_op jit(solution)/shard_map/ppermute | solution.py:16
  59.0 0.0 collective-permute-start.8
  59.0 18.3 %collective-permute-done.3.refs_0_ = bf16[256,2048]{1,0:T(8,128)(2,1)S(1)} collective-permute-done((bf16[256,2048]{1,0:T(8,128)(2,1)}, bf16[256,2048]{1,0:T(8,128)(2,1)S(1)}, u32[]{:S(2)}, u32[]{:S(2)}) %collective-permute-start.3) | collective-permute-done | bytes 1048608 | tf_op jit(solution)/shard_map/ppermute | solution.py:16
  77.3 0.0 collective-permute-done.6.refs_3_
  77.3 0.9 collective-permute-start.9
  78.2 2.1 %collective-permute-start.7 = (bf16[256,2048]{1,0:T(8,128)(2,1)S(1)}, bf16[256,2048]{1,0:T(8,128)(2,1)S(1)}, u32[]{:S(2)}, u32[]{:S(2)}) collective-permute-start(bf16[256,2048]{1,0:T(8,128)(2,1)S(1)} %collective-permute-done.3.refs_0_), channel_id=1, source_target_pairs={{4,5},{5,6},{6,7},{7,4},{12,13},{13,14},{14,15},{15,12},{20,21},{2... | collective-permute-start | bytes 3145736 | tf_op jit(solution)/shard_map/ppermute | solution.py:21
  80.3 0.0 copy-done.3
  80.3 9.7 %shard_map.38 = (f32[512,2048]{1,0:T(8,128)S(1)}, f32[512,2048]{1,0:T(8,128)S(1)}, f32[8,128]{1,0:T(8,128)S(1)}) custom-call(f32[4]{0:T(128)S(1)} %copy-done.4, f32[4]{0:T(128)S(1)} %collective-permute-done.energy_part, f32[1,128]{1,0:T(1,128)S(1)} %dynamic-slice_bitcast_fusion.virt_rows, ...), custom_call_target="tpu_custom_call", output_to_operand_aliasing={{0}: (11, {}), {1}: (12, {})} | custom-call | tf_op jit(solution)/shard_map/pallas_call | solution.py:195
  90.0 8.8 %collective-permute-done.8.refs_1_ = bf16[256,2048]{1,0:T(8,128)(2,1)S(1)} collective-permute-done((bf16[256,2048]{1,0:T(8,128)(2,1)S(1)}, bf16[256,2048]{1,0:T(8,128)(2,1)S(1)}, u32[]{:S(2)}, u32[]{:S(2)}) %collective-permute-start.8) | collective-permute-done | bytes 1048608 | tf_op jit(solution)/shard_map/ppermute | solution.py:16
  98.8 0.0 collective-permute-done.9.refs_2_
  98.8 1.9 %collective-permute-start.10 = (bf16[256,2048]{1,0:T(8,128)(2,1)S(1)}, bf16[256,2048]{1,0:T(8,128)(2,1)S(1)}, u32[]{:S(2)}, u32[]{:S(2)}) collective-permute-start(bf16[256,2048]{1,0:T(8,128)(2,1)S(1)} %collective-permute-done.8.refs_1_), channel_id=1, source_target_pairs={{0,4},{4,8},{8,12},{12,0},{1,5},{5,9},{9,13},{13,1},{2,6},{6,10},{... | collective-permute-start | bytes 3145736 | tf_op jit(solution)/shard_map/ppermute | solution.py:16
  100.7 0.7 collective-permute-start.11
  101.4 13.0 %collective-permute-done.7.refs_1_ = bf16[256,2048]{1,0:T(8,128)(2,1)S(1)} collective-permute-done((bf16[256,2048]{1,0:T(8,128)(2,1)S(1)}, bf16[256,2048]{1,0:T(8,128)(2,1)S(1)}, u32[]{:S(2)}, u32[]{:S(2)}) %collective-permute-start.7) | collective-permute-done | bytes 1048608 | tf_op jit(solution)/shard_map/ppermute | solution.py:21
  114.4 0.0 collective-permute-done.10.refs_3_
  114.4 2.5 %collective-permute-start.12 = (bf16[256,2048]{1,0:T(8,128)(2,1)S(1)}, bf16[256,2048]{1,0:T(8,128)(2,1)S(1)}, u32[]{:S(2)}, u32[]{:S(2)}) collective-permute-start(bf16[256,2048]{1,0:T(8,128)(2,1)S(1)} %collective-permute-done.7.refs_1_), channel_id=1, source_target_pairs={{4,8},{12,0},{5,9},{13,1},{6,10},{14,2},{7,11},{15,3},{20,24},{28,... | collective-permute-start | bytes 3145736 | tf_op jit(solution)/shard_map/ppermute | solution.py:30
  116.9 2.5 %collective-permute-start.15 = (bf16[256,2048]{1,0:T(8,128)(2,1)S(1)}, bf16[256,2048]{1,0:T(8,128)(2,1)S(1)}, u32[]{:S(2)}, u32[]{:S(2)}) collective-permute-start(bf16[256,2048]{1,0:T(8,128)(2,1)S(1)} %collective-permute-done.8.refs_1_), channel_id=1, source_target_pairs={{4,5},{5,6},{6,7},{7,4},{12,13},{13,14},{14,15},{15,12},{20,21},{2... | collective-permute-start | bytes 3145736 | tf_op jit(solution)/shard_map/ppermute | solution.py:21
  119.4 8.8 %shard_map.39 = (f32[512,2048]{1,0:T(8,128)S(1)}, f32[512,2048]{1,0:T(8,128)S(1)}, f32[8,128]{1,0:T(8,128)S(1)}) custom-call(f32[4]{0:T(128)S(1)} %copy-done.4, f32[4]{0:T(128)S(1)} %collective-permute-done.energy_part, f32[1,128]{1,0:T(1,128)S(1)} %dynamic-slice_bitcast_fusion.virt_rows, ...), custom_call_target="tpu_custom_call", output_to_operand_aliasing={{0}: (11, {}), {1}: (12, {})} | custom-call | tf_op jit(solution)/shard_map/pallas_call | solution.py:195
  128.2 0.0 collective-permute-done.11.refs_0_
  128.2 1.3 collective-permute-start.13
  129.5 0.0 collective-permute-done.12.refs_2_
  129.5 0.7 collective-permute-start.14
  130.2 4.0 %collective-permute-done.15.refs_1_ = bf16[256,2048]{1,0:T(8,128)(2,1)S(1)} collective-permute-done((bf16[256,2048]{1,0:T(8,128)(2,1)S(1)}, bf16[256,2048]{1,0:T(8,128)(2,1)S(1)}, u32[]{:S(2)}, u32[]{:S(2)}) %collective-permute-start.15) | collective-permute-done | bytes 1048608 | tf_op jit(solution)/shard_map/ppermute | solution.py:21
  134.2 2.0 %collective-permute-start.16 = (bf16[256,2048]{1,0:T(8,128)(2,1)S(1)}, bf16[256,2048]{1,0:T(8,128)(2,1)S(1)}, u32[]{:S(2)}, u32[]{:S(2)}) collective-permute-start(bf16[256,2048]{1,0:T(8,128)(2,1)S(1)} %collective-permute-done.15.refs_1_), channel_id=1, source_target_pairs={{4,8},{12,0},{5,9},{13,1},{6,10},{14,2},{7,11},{15,3},{20,24},{28,... | collective-permute-start | bytes 3145736 | tf_op jit(solution)/shard_map/ppermute | solution.py:30
  136.2 0.0 collective-permute-done.13.refs_3_
  136.2 5.3 %shard_map.40 = (f32[512,2048]{1,0:T(8,128)S(1)}, f32[512,2048]{1,0:T(8,128)S(1)}, f32[8,128]{1,0:T(8,128)S(1)}) custom-call(f32[4]{0:T(128)S(1)} %copy-done.4, f32[4]{0:T(128)S(1)} %collective-permute-done.energy_part, f32[1,128]{1,0:T(1,128)S(1)} %dynamic-slice_bitcast_fusion.virt_rows, ...), custom_call_target="tpu_custom_call", output_to_operand_aliasing={{0}: (11, {}), {1}: (12, {})} | custom-call | tf_op jit(solution)/shard_map/pallas_call | solution.py:195
  141.5 0.0 collective-permute-done.14.refs_0_
  141.5 1.3 collective-permute-start.17
  142.8 5.1 %collective-permute-done.16.refs_2_ = bf16[256,2048]{1,0:T(8,128)(2,1)S(1)} collective-permute-done((bf16[256,2048]{1,0:T(8,128)(2,1)S(1)}, bf16[256,2048]{1,0:T(8,128)(2,1)S(1)}, u32[]{:S(2)}, u32[]{:S(2)}) %collective-permute-start.16) | collective-permute-done | bytes 1048608 | tf_op jit(solution)/shard_map/ppermute | solution.py:30
  147.9 4.7 %collective-permute-done.17.refs_3_ = bf16[256,2048]{1,0:T(8,128)(2,1)S(1)} collective-permute-done((bf16[256,2048]{1,0:T(8,128)(2,1)S(1)}, bf16[256,2048]{1,0:T(8,128)(2,1)S(1)}, u32[]{:S(2)}, u32[]{:S(2)}) %collective-permute-start.17) | collective-permute-done | bytes 1048608 | tf_op jit(solution)/shard_map/ppermute | solution.py:30
  152.6 3.3 %shard_map.41 = (bf16[512,2048]{1,0:T(8,128)(2,1)S(1)}, f32[8,128]{1,0:T(8,128)S(1)}) custom-call(f32[4]{0:T(128)S(1)} %copy-done.4, f32[4]{0:T(128)S(1)} %collective-permute-done.energy_part, f32[1,128]{1,0:T(1,128)S(1)} %dynamic-slice_bitcast_fusion.virt_rows, f32[512,1]{1,0:T(8,128)S(1)} %copy.16.virt_column, f32[8,128]{1,0:T(8,128)S(1)} %get-tuple-element.58.after, ...), custom_call_target="tpu_custom_call" | custom-call | tf_op jit(solution)/shard_map/pallas_call | solution.py:195
  155.9 0.2 collective-permute-start.18
  156.1 4.1 %shard_map.42 = (f32[512,2048]{1,0:T(8,128)S(1)}, f32[8,128]{1,0:T(8,128)}) custom-call(f32[4]{0:T(128)S(1)} %copy-done.4, f32[4]{0:T(128)S(1)} %collective-permute-done.energy_part, f32[1,128]{1,0:T(1,128)S(1)} %dynamic-slice_bitcast_fusion.virt_rows, f32[512,1]{1,0:T(8,128)S(1)} %copy.16.virt_column, ...), custom_call_target="tpu_custom_call", output_to_operand_aliasing={{0}: (11, {})} | custom-call | tf_op jit(solution)/shard_map/pallas_call | solution.py:195
  160.2 21.2 %collective-permute-done.18 = bf16[512,2048]{1,0:T(8,128)(2,1)S(1)} collective-permute-done((bf16[512,2048]{1,0:T(8,128)(2,1)S(1)}, bf16[512,2048]{1,0:T(8,128)(2,1)S(1)}, u32[]{:S(2)}, u32[]{:S(2)}) %collective-permute-start.18) | collective-permute-done | bytes 2097184 | tf_op jit(solution)/shard_map/ppermute | solution.py:16
  181.4 2.0 %add_convert_fusion = bf16[512,2048]{1,0:T(8,128)(2,1)} fusion(f32[512,2048]{1,0:T(8,128)S(1)} %get-tuple-element.65, bf16[512,2048]{1,0:T(8,128)(2,1)S(1)} %collective-permute-done.18), kind=kLoop, calls=%fused_computation | loop fusion | flops 3145728 | bytes 8388608 | tf_op jit(solution)/shard_map/convert_element_type | solution.py:288
Async XLA Ops:
  0.0 46.8 %copy-start = (bf16[4,128,2048]{2,1,0:T(8,128)(2,1)S(1)}, bf16[4,128,2048]{2,1,0:T(8,128)(2,1)}, u32[]{:S(2)}) copy-start(bf16[4,128,2048]{2,1,0:T(8,128)(2,1)} %param.3) | copy-start | bytes 6291460
  0.0 34.7 %copy-start.4 = (f32[4]{0:T(128)S(1)}, f32[4]{0:T(128)}, u32[]{:S(2)}) copy-start(f32[4]{0:T(128)} %energy_own.11) | copy-start | bytes 52
  0.0 34.7 %copy-start.5 = (f32[512]{0:T(512)S(1)}, f32[512]{0:T(512)}, u32[]{:S(2)}) copy-start(f32[512]{0:T(512)} %param.5) | copy-start | bytes 6148
  0.0 32.4 %collective-permute-start.2 = (bf16[512,2048]{1,0:T(8,128)(2,1)}, bf16[512,2048]{1,0:T(8,128)(2,1)S(1)}, u32[]{:S(2)}, u32[]{:S(2)}) collective-permute-start(bf16[512,2048]{1,0:T(8,128)(2,1)} %bitcast.7), channel_id=1, source_target_pairs={{0,4},{4,8},{8,12},{12,0},{1,5},{5,9},{9,13},{13,1},{2,6},{6,10},{... | collective-permute-start | bytes 6291464 | tf_op jit(solution)/shard_map/ppermute | solution.py:16
  5.4 27.0 %collective-permute-start.1 = (bf16[256,2048]{1,0:T(8,128)(2,1)S(1)}, bf16[256,2048]{1,0:T(8,128)(2,1)}, u32[]{:S(2)}, u32[]{:S(2)}) collective-permute-start(bf16[256,2048]{1,0:T(8,128)(2,1)S(1)} %bitcast.15), channel_id=1, source_target_pairs={{0,1},{1,2},{2,3},{3,0},{4,5},{5,6},{6,7},{7,4},{8,9},{9,10},{10,1... | collective-permute-start | bytes 3145736 | tf_op jit(solution)/shard_map/ppermute | solution.py:16
  6.7 49.8 %collective-permute-start.4 = (bf16[256,2048]{1,0:T(8,128)(2,1)}, bf16[256,2048]{1,0:T(8,128)(2,1)S(1)}, u32[]{:S(2)}, u32[]{:S(2)}) collective-permute-start(bf16[256,2048]{1,0:T(8,128)(2,1)} %bitcast.3), channel_id=1, source_target_pairs={{0,1},{1,2},{2,3},{3,0},{4,5},{5,6},{6,7},{7,4},{8,9},{9,10},{10,1... | collective-permute-start | bytes 3145736 | tf_op jit(solution)/shard_map/ppermute | solution.py:16
  32.4 1.3 copy-start.1
  33.7 22.8 %collective-permute-start.5 = (bf16[256,2048]{1,0:T(8,128)(2,1)}, bf16[256,2048]{1,0:T(8,128)(2,1)}, u32[]{:S(2)}, u32[]{:S(2)}) collective-permute-start(bf16[256,2048]{1,0:T(8,128)(2,1)} %collective-permute-done.1.refs_0_), channel_id=1, source_target_pairs={{0,4},{4,8},{8,12},{12,0},{1,5},{5,9},{9,13},{13,1},{2,6},{6,10},{... | collective-permute-start | bytes 3145736 | tf_op jit(solution)/shard_map/ppermute | solution.py:16
  34.7 12.1 %collective-permute-start = (f32[4]{0:T(128)S(1)}, f32[4]{0:T(128)S(1)}, u32[]{:S(2)}, u32[]{:S(2)}) collective-permute-start(f32[4]{0:T(128)S(1)} %copy-done.4), channel_id=1, source_target_pairs={{0,4},{4,8},{8,12},{12,0},{1,5},{5,9},{9,13},{13,1},{2,6},{6,10},{... | collective-permute-start | bytes 56 | tf_op jit(solution)/shard_map/ppermute | solution.py:16
  35.0 42.4 %collective-permute-start.3 = (bf16[256,2048]{1,0:T(8,128)(2,1)}, bf16[256,2048]{1,0:T(8,128)(2,1)S(1)}, u32[]{:S(2)}, u32[]{:S(2)}) collective-permute-start(bf16[256,2048]{1,0:T(8,128)(2,1)} %collective-permute-done.1.refs_0_), channel_id=1, source_target_pairs={{0,1},{1,2},{2,3},{3,0},{4,5},{5,6},{6,7},{7,4},{8,9},{9,10},{10,1... | collective-permute-start | bytes 3145736 | tf_op jit(solution)/shard_map/ppermute | solution.py:16
  46.8 1.6 copy-start.2
  48.4 32.0 %copy-start.3 = (bf16[512,2048]{1,0:T(8,128)(2,1)S(1)}, bf16[512,2048]{1,0:T(8,128)(2,1)}, u32[]{:S(2)}) copy-start(bf16[512,2048]{1,0:T(8,128)(2,1)} %copy-done.1) | copy-start | bytes 6291460
  56.5 20.8 %collective-permute-start.6 = (bf16[256,2048]{1,0:T(8,128)(2,1)S(1)}, bf16[256,2048]{1,0:T(8,128)(2,1)S(1)}, u32[]{:S(2)}, u32[]{:S(2)}) collective-permute-start(bf16[256,2048]{1,0:T(8,128)(2,1)S(1)} %collective-permute-done.4.refs_1_), channel_id=1, source_target_pairs={{0,4},{4,8},{8,12},{12,0},{1,5},{5,9},{9,13},{13,1},{2,6},{6,10},{... | collective-permute-start | bytes 3145736 | tf_op jit(solution)/shard_map/ppermute | solution.py:16
  59.0 39.8 %collective-permute-start.8 = (bf16[256,2048]{1,0:T(8,128)(2,1)S(1)}, bf16[256,2048]{1,0:T(8,128)(2,1)S(1)}, u32[]{:S(2)}, u32[]{:S(2)}) collective-permute-start(bf16[256,2048]{1,0:T(8,128)(2,1)S(1)} %collective-permute-done.4.refs_1_), channel_id=1, source_target_pairs={{0,1},{1,2},{2,3},{3,0},{4,5},{5,6},{6,7},{7,4},{8,9},{9,10},{10,1... | collective-permute-start | bytes 3145736 | tf_op jit(solution)/shard_map/ppermute | solution.py:16
  77.3 21.4 %collective-permute-start.9 = (bf16[256,2048]{1,0:T(8,128)(2,1)S(1)}, bf16[256,2048]{1,0:T(8,128)(2,1)S(1)}, u32[]{:S(2)}, u32[]{:S(2)}) collective-permute-start(bf16[256,2048]{1,0:T(8,128)(2,1)S(1)} %collective-permute-done.3.refs_0_), channel_id=1, source_target_pairs={{0,4},{4,8},{8,12},{12,0},{1,5},{5,9},{9,13},{13,1},{2,6},{6,10},{... | collective-permute-start | bytes 3145736 | tf_op jit(solution)/shard_map/ppermute | solution.py:16
  78.2 36.2 %collective-permute-start.7 = (bf16[256,2048]{1,0:T(8,128)(2,1)S(1)}, bf16[256,2048]{1,0:T(8,128)(2,1)S(1)}, u32[]{:S(2)}, u32[]{:S(2)}) collective-permute-start(bf16[256,2048]{1,0:T(8,128)(2,1)S(1)} %collective-permute-done.3.refs_0_), channel_id=1, source_target_pairs={{4,5},{5,6},{6,7},{7,4},{12,13},{13,14},{14,15},{15,12},{20,21},{2... | collective-permute-start | bytes 3145736 | tf_op jit(solution)/shard_map/ppermute | solution.py:21
  98.8 15.6 %collective-permute-start.10 = (bf16[256,2048]{1,0:T(8,128)(2,1)S(1)}, bf16[256,2048]{1,0:T(8,128)(2,1)S(1)}, u32[]{:S(2)}, u32[]{:S(2)}) collective-permute-start(bf16[256,2048]{1,0:T(8,128)(2,1)S(1)} %collective-permute-done.8.refs_1_), channel_id=1, source_target_pairs={{0,4},{4,8},{8,12},{12,0},{1,5},{5,9},{9,13},{13,1},{2,6},{6,10},{... | collective-permute-start | bytes 3145736 | tf_op jit(solution)/shard_map/ppermute | solution.py:16
  100.7 27.5 %collective-permute-start.11 = (bf16[256,2048]{1,0:T(8,128)(2,1)S(1)}, bf16[256,2048]{1,0:T(8,128)(2,1)S(1)}, u32[]{:S(2)}, u32[]{:S(2)}) collective-permute-start(bf16[256,2048]{1,0:T(8,128)(2,1)S(1)} %collective-permute-done.3.refs_0_), channel_id=1, source_target_pairs={{0,1},{1,2},{2,3},{3,0},{8,9},{9,10},{10,11},{11,8},{16,17},{17,18... | collective-permute-start | bytes 3145736 | tf_op jit(solution)/shard_map/ppermute | solution.py:21
  114.4 15.1 %collective-permute-start.12 = (bf16[256,2048]{1,0:T(8,128)(2,1)S(1)}, bf16[256,2048]{1,0:T(8,128)(2,1)S(1)}, u32[]{:S(2)}, u32[]{:S(2)}) collective-permute-start(bf16[256,2048]{1,0:T(8,128)(2,1)S(1)} %collective-permute-done.7.refs_1_), channel_id=1, source_target_pairs={{4,8},{12,0},{5,9},{13,1},{6,10},{14,2},{7,11},{15,3},{20,24},{28,... | collective-permute-start | bytes 3145736 | tf_op jit(solution)/shard_map/ppermute | solution.py:30
  116.9 17.3 %collective-permute-start.15 = (bf16[256,2048]{1,0:T(8,128)(2,1)S(1)}, bf16[256,2048]{1,0:T(8,128)(2,1)S(1)}, u32[]{:S(2)}, u32[]{:S(2)}) collective-permute-start(bf16[256,2048]{1,0:T(8,128)(2,1)S(1)} %collective-permute-done.8.refs_1_), channel_id=1, source_target_pairs={{4,5},{5,6},{6,7},{7,4},{12,13},{13,14},{14,15},{15,12},{20,21},{2... | collective-permute-start | bytes 3145736 | tf_op jit(solution)/shard_map/ppermute | solution.py:21
  128.2 8.0 %collective-permute-start.13 = (bf16[256,2048]{1,0:T(8,128)(2,1)S(1)}, bf16[256,2048]{1,0:T(8,128)(2,1)S(1)}, u32[]{:S(2)}, u32[]{:S(2)}) collective-permute-start(bf16[256,2048]{1,0:T(8,128)(2,1)S(1)} %collective-permute-done.11.refs_0_), channel_id=1, source_target_pairs={{0,4},{8,12},{1,5},{9,13},{2,6},{10,14},{3,7},{11,15},{16,20},{24,... | collective-permute-start | bytes 3145736 | tf_op jit(solution)/shard_map/ppermute | solution.py:30
  129.5 12.0 %collective-permute-start.14 = (bf16[256,2048]{1,0:T(8,128)(2,1)S(1)}, bf16[256,2048]{1,0:T(8,128)(2,1)S(1)}, u32[]{:S(2)}, u32[]{:S(2)}) collective-permute-start(bf16[256,2048]{1,0:T(8,128)(2,1)S(1)} %collective-permute-done.8.refs_1_), channel_id=1, source_target_pairs={{0,1},{1,2},{2,3},{3,0},{8,9},{9,10},{10,11},{11,8},{16,17},{17,18... | collective-permute-start | bytes 3145736 | tf_op jit(solution)/shard_map/ppermute | solution.py:21
  134.2 13.7 %collective-permute-start.16 = (bf16[256,2048]{1,0:T(8,128)(2,1)S(1)}, bf16[256,2048]{1,0:T(8,128)(2,1)S(1)}, u32[]{:S(2)}, u32[]{:S(2)}) collective-permute-start(bf16[256,2048]{1,0:T(8,128)(2,1)S(1)} %collective-permute-done.15.refs_1_), channel_id=1, source_target_pairs={{4,8},{12,0},{5,9},{13,1},{6,10},{14,2},{7,11},{15,3},{20,24},{28,... | collective-permute-start | bytes 3145736 | tf_op jit(solution)/shard_map/ppermute | solution.py:30
  141.5 11.1 %collective-permute-start.17 = (bf16[256,2048]{1,0:T(8,128)(2,1)S(1)}, bf16[256,2048]{1,0:T(8,128)(2,1)S(1)}, u32[]{:S(2)}, u32[]{:S(2)}) collective-permute-start(bf16[256,2048]{1,0:T(8,128)(2,1)S(1)} %collective-permute-done.14.refs_0_), channel_id=1, source_target_pairs={{0,4},{8,12},{1,5},{9,13},{2,6},{10,14},{3,7},{11,15},{16,20},{24,... | collective-permute-start | bytes 3145736 | tf_op jit(solution)/shard_map/ppermute | solution.py:30
  155.9 25.5 %collective-permute-start.18 = (bf16[512,2048]{1,0:T(8,128)(2,1)S(1)}, bf16[512,2048]{1,0:T(8,128)(2,1)S(1)}, u32[]{:S(2)}, u32[]{:S(2)}) collective-permute-start(bf16[512,2048]{1,0:T(8,128)(2,1)S(1)} %get-tuple-element.66), channel_id=1, source_target_pairs={{0,12},{4,0},{8,4},{12,8},{1,13},{5,1},{9,5},{13,9},{2,14},{6,2},{... | collective-permute-start | bytes 6291464 | tf_op jit(solution)/shard_map/ppermute | solution.py:16

commit v3 on v2

--- a/solution.py
+++ b/solution.py
@@ -46,14 +46,16 @@
     return lax.rem(lax.axis_index("virt") + (steps - step), steps) * here + begin
 
 
-def tile_plain(rows, tile, energies, sums, want, span):
+def tile_plain(rows, tile, energies, sums, want, spans):
     own_rows, part_rows = rows
     own_tile, part_tile = tile
     energy_own, energy_part, virt_rows, virt_column = energies
     occ, here = energy_own.shape[0], virt_rows.shape[1]
     there = own_tile.shape[0] // occ
     virt_rows = virt_rows[0]
-    virt_tile = lax.dynamic_slice_in_dim(virt_column[:, 0], first_row(span, here), there, 0)
+    virt_tile = jnp.concatenate([
+        lax.dynamic_slice_in_dim(virt_column[:, 0], first_row(span, here), size, 0) for span, size in spans
+    ])
     shape = (occ, there, occ, here)
     diag = contract(own_tile, own_rows).reshape(shape)
     first = contract(part_tile, own_rows).reshape(shape)
@@ -82,7 +84,7 @@
 
 
 def tile_kernel(
-    occ, here, sizes, choices, columns, want, summed, span, energy_own, energy_part, virt_rows, virt_column,
+    occ, here, sizes, choices, windows, want, summed, spans, energy_own, energy_part, virt_rows, virt_column,
     after, own_rows, part_rows, *refs,
 ):
     del after
@@ -125,8 +127,9 @@
     for copies in groups[1]:
         copies[0].wait()
     first[...] = contract(tiles[wide:], own_rows[...])
-    begin = pl.multiple_of(first_row(span, here), 16)
-    virt = virt_column[pl.ds(begin, there)] + virt_rows[...]
+    virt = jnp.concatenate([
+        virt_column[pl.ds(pl.multiple_of(first_row(span, here), 16), size)] for span, size in zip(spans, sizes)
+    ]) + virt_rows[...]
 
     def block(ref, r, c):
         return ref[r * there:(r + 1) * there, c * here:(c + 1) * here]
@@ -153,9 +156,10 @@
                 for i in range(occ)
             ], j)
 
-    for begin in range(0, tiles.shape[1], columns):
-        at = slice(begin, begin + columns)
-        for name, total, out in zip(want, sums, outs):
+    for name, total, out, window in zip(want, sums, outs, windows):
+        columns = min(window[1] - window[0], 512)
+        for begin in range(*window, columns):
+            at = slice(begin, begin + columns)
             if name == "own":
                 term = jnp.dot(left[:, :2 * wide], tiles[:, at], preferred_element_type=jnp.float32)
             else:
@@ -163,10 +167,11 @@
                 term = jnp.dot(
                     left[:, skip:skip + wide], tiles[:wide, at], preferred_element_type=jnp.float32
                 )
-            out[:, at] = (term if total is None else total[:, at] + term).astype(out.dtype)
-
-
-def tile_terms(rows, pieces, energies, sums, want, span, after, kinds=None):
+            term = term if total is None else total[:, at] + term
+            out[:, begin - window[0]:begin - window[0] + columns] = term.astype(out.dtype)
+
+
+def tile_terms(rows, pieces, energies, sums, want, spans, after, kinds=None, windows=None):
     energy_own, virt_rows = energies[0], energies[2]
     occ, here = energy_own.shape[0], virt_rows.shape[1]
     aux = rows[0].shape[1]
@@ -181,10 +186,12 @@
             jnp.concatenate([p.reshape(occ, -1, aux) for p in side], axis=1).reshape(occ * there, aux)
             for side in chosen
         ]
-        sums = [t.astype(k) for t, k in zip(tile_plain(rows, tile, energies, sums, want, span), kinds)]
+        terms = tile_plain(rows, tile, energies, sums, want, list(zip(spans, sizes)))
+        windows = windows or ((0, aux),) * len(want)
+        sums = [t[:, slice(*window)].astype(k) for t, k, window in zip(terms, kinds, windows)]
         return *sums, sums[0][:1, :1]
     flat_pieces = [p for side in pieces for choice in side for p in choice]
-    columns = min(aux, 512)
+    windows = windows or ((0, aux),) * len(want)
     wide, tall = occ * there, occ * here
     summed = sums[0] is not None
     scalar = pl.BlockSpec(memory_space=pltpu.SMEM)
@@ -193,12 +200,13 @@
     products = 3 if "own" in want else 2
     spreads = (2 if "own" in want else 0) + (1 if "partner" in want else 0)
     return pl.pallas_call(
-        functools.partial(tile_kernel, occ, here, sizes, choices, columns, want, summed, span),
+        functools.partial(tile_kernel, occ, here, sizes, choices, windows, want, summed, spans),
         in_specs=[scalar, scalar, vmem, vmem, hbm, vmem, vmem] + [hbm] * len(flat_pieces) + [vmem] * (len(want) * summed),
         out_specs=[vmem] * (len(want) + 1),
         out_shape=[
-            pltpu.VMEM((tall, aux), kind) if kind == jnp.float32 else jax.ShapeDtypeStruct((tall, aux), kind)
-            for kind in kinds
+            pltpu.VMEM((tall, aux), kind) if kind == jnp.float32
+            else jax.ShapeDtypeStruct((tall, window[1] - window[0]), kind)
+            for kind, window in zip(kinds, windows)
         ] + [jax.ShapeDtypeStruct((8, LANES), jnp.float32)],
         input_output_aliases={
             7 + len(flat_pieces) + n: n for n, kind in enumerate(kinds) if summed and kind == jnp.float32
@@ -218,13 +226,55 @@
     )
 
 
+def finish_kernel(window, begins, own, *refs):
+    backs, (out, scratch, sem) = refs[:len(begins)], refs[-3:]
+    tall, width = scratch.shape
+    strip = tall // sem.shape[0]
+    copies = []
+    for n in range(sem.shape[0]):
+        at = slice(n * strip, (n + 1) * strip)
+        total = own[at, window[0]:window[1]]
+        for back, begin in zip(backs, begins):
+            start = window[0] - begin
+            total = total + back[at, start:start + width].astype(jnp.float32)
+        scratch[at] = total.astype(scratch.dtype)
+        copies.append(pltpu.make_async_copy(scratch.at[at], out.at[at, pl.ds(window[0], width)], sem.at[n]))
+        copies[-1].start()
+    for copy in copies:
+        copy.wait()
+
+
+def finished(own, backs, windows):
+    tall, aux = own.shape
+    if tall % LANES:
+        return sum((back.astype(jnp.float32) for back, _ in backs), start=own).astype(jnp.bfloat16)
+    out = None
+    vmem, hbm = pl.BlockSpec(memory_space=pltpu.VMEM), pl.BlockSpec(memory_space=pl.ANY)
+    for window in windows:
+        near = [(back, span[0]) for back, span in backs if span[0] <= window[0] and window[1] <= span[1]]
+        done = [] if out is None else [out]
+        out = pl.pallas_call(
+            functools.partial(finish_kernel, window, [begin for _, begin in near]),
+            in_specs=[vmem] * (1 + len(near)) + [hbm] * len(done),
+            out_specs=hbm,
+            out_shape=jax.ShapeDtypeStruct((tall, aux), jnp.bfloat16),
+            input_output_aliases={1 + len(near): 0} if done else {},
+            scratch_shapes=[
+                pltpu.VMEM((tall, window[1] - window[0]), jnp.bfloat16),
+                pltpu.SemaphoreType.DMA((4,)),
+            ],
+            compiler_params=pltpu.CompilerParams(vmem_limit_bytes=VMEM_BYTES),
+            cost_estimate=pl.CostEstimate(flops=0, bytes_accessed=0, transcendentals=0),
+        )(own, *(back for back, _ in near), *done)
+    return out
+
+
 def local(three_index, occ_energy, virt_energy):
     occ, here, aux = three_index.shape
     steps = lax.axis_size("virt")
     me = lax.axis_index("virt")
     sizes = (here // 2,) * 2 if here % LANES == 0 else (here,)
     offsets = [sum(sizes[:c]) for c in range(len(sizes))]
-    cut = len(sizes) // 2
     energy_part = shifted(occ_energy, "blk", 1)
     virt_rows = lax.dynamic_slice_in_dim(virt_energy, me * here, here, 0)
     own_rows = three_index.reshape(occ * here, aux)
@@ -235,17 +285,19 @@
     energies = (occ_energy, energy_part, virt_rows[None, :], virt_energy[:, None])
     done = jnp.zeros((1, 1), jnp.float32)
 
-    def terms(step, pieces, sums, want, begin, after, kinds=None):
+    def terms(runs, pieces, sums, want, after, kinds=None, windows=None):
         after, _ = lax.optimization_barrier((done, after))
-        *sums, end = tile_terms(rows, pieces, energies, sums, want, (step, begin), after, kinds)
+        spans = [(step, offsets[c]) for step, c in runs]
+        *sums, end = tile_terms(rows, pieces, energies, sums, want, spans, after, kinds, windows)
         return sums, end
 
     tiles = lax.optimization_barrier([
         three_index[:, o:o + size].reshape(occ * size, aux) for o, size in zip(offsets, sizes)
     ])
-    ordered = lax.axis_size("blk") % 2 == 0 and cut > 0 and steps > 2
+    ordered = lax.axis_size("blk") % 2 == 0 and len(sizes) == 2 and steps > 2
     moving = [shifted(tile, "virt", 1) for tile in tiles]
-    waiting = ([own_rows], [part_rows])
+    count = len(sizes)
+    waiting, runs = ([own_rows], [part_rows]), [(0, 0)]
     sums = (None, None)
     for step in range(1, steps - ordered):
         tiles, later, parts = [], [], []
@@ -258,34 +310,38 @@
                 later.append(around(tile, 1))
             parts.append(shifted(tile, "blk", 1))
             if c == 0:
-                sums, done = terms(step - 1, waiting, sums, both, 0, tile)
-        waiting, moving = (tiles, parts), later
+                sums, done = terms(runs, waiting, sums, both, tile)
+            elif ordered and step == steps - 2:
+                sums, done = terms([(step, 0)], (tiles[:1], parts[:1]), sums, both, tile)
+        waiting, moving, runs = (tiles, parts), later, [(step, c) for c in range(count)]
     step = steps - 1
     if ordered:
-        crossed, behind = [], []
-        for c, tile in enumerate(moving):
-            tile, *_ = lax.optimization_barrier((tile, done, (crossed or parts)[-1]))
-            moving[c] = tile
-            crossed.append(passed(tile, 1, 1))
-            if c == 0:
-                sums, done = terms(step - 1, waiting, sums, both, 0, tile)
-            held = tiles[c]
-            if c:
-                held, _ = lax.optimization_barrier((held, crossed[c - 1]))
-            behind.append(around(held, 0))
-        tiles, parts = [], []
-        for c, tile in enumerate(behind):
-            tile, _ = lax.optimization_barrier((tile, done))
-            tiles.append((tile, moving[c]))
-            parts.append((crossed[c], passed(tile, 0, 1)))
-            if c + 1 == cut:
-                sums, done = terms(step, (tiles[:cut], parts[:cut]), sums, both, 0, tile)
-    begin = offsets[cut]
-    tail = (tiles[cut:], parts[cut:])
-    (partner,), done = terms(step, tail, sums[1:], ("partner",), begin, done, (jnp.bfloat16,))
-    back = shifted(partner, "blk", -1)
-    (own,), done = terms(step, tail, sums[:1], ("own",), begin, done)
-    return (own + back.astype(jnp.float32)).astype(jnp.bfloat16).reshape(occ, here, aux)
+        first, second = moving
+        first, *_ = lax.optimization_barrier((first, done, parts[1]))
+        crossed = [passed(first, 1, 1)]
+        behind = [around(tiles[0], 0)]
+        second, held, _ = lax.optimization_barrier((second, tiles[1], crossed[0]))
+        crossed.append(passed(second, 1, 1))
+        behind.append(around(held, 0))
+        beside = [passed(behind[0], 0, 1)]
+        early = ([tiles[1], (behind[0], first)], [parts[1], (crossed[0], beside[0])])
+        sums, done = terms([(step - 1, 1), (step, 0)], early, sums, both, second)
+        windows, runs = ((0, aux),), [(step, 1)]
+        chosen = ([behind[1]], [crossed[1]])
+        (partner,), done = terms(runs, chosen, sums[1:], ("partner",), done, (jnp.bfloat16,))
+        backs = [(passed(partner, 0, -1), windows[0])]
+        late, _ = lax.optimization_barrier((behind[1], done))
+        beside.append(passed(late, 0, 1))
+        tail = ([(late, second)], [(crossed[1], beside[1])])
+        chosen = ([second], [beside[1]])
+        (partner,), done = terms(runs, chosen, sums[1:], ("partner",), done, (jnp.bfloat16,))
+        backs.append((passed(partner, 1, -1), windows[0]))
+    else:
+        windows, tail = [(0, aux)], waiting
+        (partner,), done = terms(runs, tail, sums[1:], ("partner",), done, (jnp.bfloat16,))
+        backs = [(shifted(partner, "blk", -1), windows[0])]
+    (own,), done = terms(runs, tail, sums[:1], ("own",), done)
+    return finished(own, backs, windows).reshape(occ, here, aux)
 
 
 def solution(mesh):

time: 184 us -> 182 us (0.989)
  waiting for transfers between devices: 111 us -> 103 us
  Pallas kernels: 39.2 us -> 44.1 us
  starting transfers between devices: 24.9 us -> 28.1 us
  other arithmetic: 2.04 us -> 0 us
    ppermute x11 -> x10, waiting for transfers between devices: 84.5 us -> 63.2 us  [shifted(): lax.ppermute(shard, axis, [(i, (i + by) % devices) for i in range(devices)])]
    ppermute x4 -> x6, waiting for transfers between devices: 9.78 us -> 19.6 us  [passed(): lax.ppermute(shard, 'blk', [(g, (g + by) % groups) for g in range(odd, gr...]
    ppermute x4 -> x6, starting transfers between devices: 7.07 us -> 11.1 us  [passed(): lax.ppermute(shard, 'blk', [(g, (g + by) % groups) for g in range(odd, gr...]
    pallas_call x6 -> x7, Pallas kernels: 39.2 us -> 42.6 us  [tile_terms(): pl.pallas_call(functools.partial(tile_kernel, occ, here, sizes, choices,...]
    ppermute x4, waiting for transfers between devices: 17 us -> 20.1 us  [around(): lax.ppermute(shard, ('blk', 'virt'), [(g * devices + i, g * devices + (i...]
    convert_element_type x1 -> x0, other arithmetic: 2.04 us -> none  [local(): (own + back.astype(jnp.float32)).astype(jnp.bfloat16)]
    ppermute x11 -> x10, starting transfers between devices: 11.8 us -> 11.6 us  [shifted(): lax.ppermute(shard, axis, [(i, (i + by) % devices) for i in range(devices)])]
  transfers between devices with their start and end apart: 19 -> 20, of which waited for: 9 -> 9; matrix products, arithmetic and copies ran while one was open for 2% -> 2% of each run, Pallas kernels for 20% -> 22%
where the time goes in v3:
time: 182 us; the launch traced here: 181 us
  waiting for transfers between devices  103 us (57%)
  Pallas kernels  44.1 us (24%)
  starting transfers between devices  28.1 us (15%)
  local copies, waits for them, and re-layouts  5.85 us (3%)
    ppermute x10, waiting for transfers between devices, shifted(): lax.ppermute(shard, axis, [(i, (i + by) % devices) for i in range(devices)])  63.2 us
    pallas_call x7, Pallas kernels, tile_terms(): pl.pallas_call(functools.partial(tile_kernel, occ, here, sizes, choices,...  42.6 us
    ppermute x4, waiting for transfers between devices, around(): lax.ppermute(shard, ('blk', 'virt'), [(g * devices + i, g * devices + (i...  20.1 us
    ppermute x6, waiting for transfers between devices, passed(): lax.ppermute(shard, 'blk', [(g, (g + by) % groups) for g in range(odd, gr...  19.6 us
    ppermute x10, starting transfers between devices, shifted(): lax.ppermute(shard, axis, [(i, (i + by) % devices) for i in range(devices)])  11.6 us
    ppermute x6, starting transfers between devices, passed(): lax.ppermute(shard, 'blk', [(g, (g + by) % groups) for g in range(odd, gr...  11.1 us
    ppermute x4, starting transfers between devices, around(): lax.ppermute(shard, ('blk', 'virt'), [(g * devices + i, g * devices + (i...  5.44 us
  transfers between devices with their start and end apart: 20, of which 9 were waited for; matrix products, arithmetic and copies ran while one was open for 2% of the time, Pallas kernels for 22%

profile of v3, /device:TPU:1, one launch (start us, length us, event | category | flops | bytes accessed | tf_op | source)
XLA Modules:
  0.0 181.4 jit_solution(564823872839312073)
XLA Ops:
  0.0 0.0 copy-start
  0.0 0.0 copy-start.3
  0.0 0.0 copy-start.4
  0.0 2.7 %collective-permute-start.2 = (bf16[512,2048]{1,0:T(8,128)(2,1)}, bf16[512,2048]{1,0:T(8,128)(2,1)S(1)}, u32[]{:S(2)}, u32[]{:S(2)}) collective-permute-start(bf16[512,2048]{1,0:T(8,128)(2,1)} %bitcast.7), channel_id=1, source_target_pairs={{0,4},{4,8},{8,12},{12,0},{1,5},{5,9},{9,13},{13,1},{2,6},{6,10},{... | collective-permute-start | bytes 6291464 | tf_op jit(solution)/shard_map/ppermute | solution.py:16
  2.7 2.7 %fusion = (bf16[4,64,2048]{2,1,0:T(8,128)(2,1)}, bf16[4,64,2048]{2,1,0:T(8,128)(2,1)S(1)}) fusion(bf16[4,128,2048]{2,1,0:T(8,128)(2,1)} %param.3), kind=kLoop, calls=%fused_computation.1 | loop fusion | bytes 4194304 | tf_op jit(solution)/shard_map/slice | solution.py:295
  5.4 1.3 collective-permute-start.1
  6.7 1.3 collective-permute-start.4
  8.0 24.4 %collective-permute-done.1.refs_0_ = bf16[256,2048]{1,0:T(8,128)(2,1)} collective-permute-done((bf16[256,2048]{1,0:T(8,128)(2,1)S(1)}, bf16[256,2048]{1,0:T(8,128)(2,1)}, u32[]{:S(2)}, u32[]{:S(2)}) %collective-permute-start.1) | collective-permute-done | bytes 1048608 | tf_op jit(solution)/shard_map/ppermute | solution.py:16
  32.4 0.0 collective-permute-done.2.part_rows.refs_1_
  32.4 0.0 copy-start.1
  32.4 1.3 copy-done.1
  33.7 1.0 collective-permute-start.5
  34.7 0.0 copy-done.3
  34.7 0.0 collective-permute-start
  34.7 0.0 copy-done.4
  34.7 0.1 copy.17.virt_column
  34.9 0.1 dynamic-slice_bitcast_fusion.virt_rows
  35.0 0.0 collective-permute-start.3
  35.0 11.8 %collective-permute-done.energy_part = f32[4]{0:T(128)S(1)} collective-permute-done((f32[4]{0:T(128)S(1)}, f32[4]{0:T(128)S(1)}, u32[]{:S(2)}, u32[]{:S(2)}) %collective-permute-start) | collective-permute-done | bytes 48 | tf_op jit(solution)/shard_map/ppermute | solution.py:16
  46.8 0.0 copy-done
  46.8 0.0 copy-start.2
  46.8 1.6 copy-done.2
  48.3 8.0 %shard_map.37 = (f32[512,2048]{1,0:T(8,128)S(1)}, f32[512,2048]{1,0:T(8,128)S(1)}, f32[8,128]{1,0:T(8,128)S(1)}) custom-call(f32[4]{0:T(128)S(1)} %copy-done.3, f32[4]{0:T(128)S(1)} %collective-permute-done.energy_part, f32[1,128]{1,0:T(1,128)S(1)} %dynamic-slice_bitcast_fusion.virt_rows, f32[512,1]{1,0:T(8,128)S(1)} %copy.17.virt_column, ...), custom_call_target="tpu_custom_call" | custom-call | tf_op jit(solution)/shard_map/pallas_call | solution.py:202
  56.4 0.0 collective-permute-done.4.refs_1_
  56.4 0.0 collective-permute-done.5.refs_2_
  56.4 2.5 %collective-permute-start.6 = (bf16[256,2048]{1,0:T(8,128)(2,1)S(1)}, bf16[256,2048]{1,0:T(8,128)(2,1)S(1)}, u32[]{:S(2)}, u32[]{:S(2)}) collective-permute-start(bf16[256,2048]{1,0:T(8,128)(2,1)S(1)} %collective-permute-done.4.refs_1_), channel_id=1, source_target_pairs={{0,4},{4,8},{8,12},{12,0},{1,5},{5,9},{9,13},{13,1},{2,6},{6,10},{... | collective-permute-start | bytes 3145736 | tf_op jit(solution)/shard_map/ppermute | solution.py:16
  59.0 0.0 collective-permute-start.7
  59.0 18.4 %collective-permute-done.3.refs_0_ = bf16[256,2048]{1,0:T(8,128)(2,1)S(1)} collective-permute-done((bf16[256,2048]{1,0:T(8,128)(2,1)}, bf16[256,2048]{1,0:T(8,128)(2,1)S(1)}, u32[]{:S(2)}, u32[]{:S(2)}) %collective-permute-start.3) | collective-permute-done | bytes 1048608 | tf_op jit(solution)/shard_map/ppermute | solution.py:16
  77.3 0.0 collective-permute-done.6.refs_3_
  77.3 0.9 collective-permute-start.8
  78.2 2.1 %collective-permute-start.10 = (bf16[256,2048]{1,0:T(8,128)(2,1)S(1)}, bf16[256,2048]{1,0:T(8,128)(2,1)S(1)}, u32[]{:S(2)}, u32[]{:S(2)}) collective-permute-start(bf16[256,2048]{1,0:T(8,128)(2,1)S(1)} %collective-permute-done.3.refs_0_), channel_id=1, source_target_pairs={{4,5},{5,6},{6,7},{7,4},{12,13},{13,14},{14,15},{15,12},{20,21},{2... | collective-permute-start | bytes 3145736 | tf_op jit(solution)/shard_map/ppermute | solution.py:21
  80.3 9.8 %shard_map.38 = (f32[512,2048]{1,0:T(8,128)S(1)}, f32[512,2048]{1,0:T(8,128)S(1)}, f32[8,128]{1,0:T(8,128)S(1)}) custom-call(f32[4]{0:T(128)S(1)} %copy-done.3, f32[4]{0:T(128)S(1)} %collective-permute-done.energy_part, f32[1,128]{1,0:T(1,128)S(1)} %dynamic-slice_bitcast_fusion.virt_rows, ...), custom_call_target="tpu_custom_call", output_to_operand_aliasing={{0}: (11, {}), {1}: (12, {})} | custom-call | tf_op jit(solution)/shard_map/pallas_call | solution.py:202
  90.1 8.7 %collective-permute-done.7.refs_0_ = bf16[256,2048]{1,0:T(8,128)(2,1)S(1)} collective-permute-done((bf16[256,2048]{1,0:T(8,128)(2,1)S(1)}, bf16[256,2048]{1,0:T(8,128)(2,1)S(1)}, u32[]{:S(2)}, u32[]{:S(2)}) %collective-permute-start.7) | collective-permute-done | bytes 1048608 | tf_op jit(solution)/shard_map/ppermute | solution.py:16
  98.8 0.0 collective-permute-done.8.refs_1_
  98.8 1.9 %collective-permute-start.11 = (bf16[256,2048]{1,0:T(8,128)(2,1)S(1)}, bf16[256,2048]{1,0:T(8,128)(2,1)S(1)}, u32[]{:S(2)}, u32[]{:S(2)}) collective-permute-start(bf16[256,2048]{1,0:T(8,128)(2,1)S(1)} %collective-permute-done.7.refs_0_), channel_id=1, source_target_pairs={{0,4},{4,8},{8,12},{12,0},{1,5},{5,9},{9,13},{13,1},{2,6},{6,10},{... | collective-permute-start | bytes 3145736 | tf_op jit(solution)/shard_map/ppermute | solution.py:16
  100.7 0.7 collective-permute-start.13
  101.4 1.9 %collective-permute-start.9 = (bf16[256,2048]{1,0:T(8,128)(2,1)S(1)}, bf16[256,2048]{1,0:T(8,128)(2,1)S(1)}, u32[]{:S(2)}, u32[]{:S(2)}) collective-permute-start(bf16[256,2048]{1,0:T(8,128)(2,1)S(1)} %collective-permute-done.7.refs_0_), channel_id=1, source_target_pairs={{4,5},{5,6},{6,7},{7,4},{12,13},{13,14},{14,15},{15,12},{20,21},{2... | collective-permute-start | bytes 3145736 | tf_op jit(solution)/shard_map/ppermute | solution.py:21
  103.3 5.3 %shard_map.39 = (f32[512,2048]{1,0:T(8,128)S(1)}, f32[512,2048]{1,0:T(8,128)S(1)}, f32[8,128]{1,0:T(8,128)S(1)}) custom-call(f32[4]{0:T(128)S(1)} %copy-done.3, f32[4]{0:T(128)S(1)} %collective-permute-done.energy_part, f32[1,128]{1,0:T(1,128)S(1)} %dynamic-slice_bitcast_fusion.virt_rows, ...), custom_call_target="tpu_custom_call", output_to_operand_aliasing={{0}: (9, {}), {1}: (10, {})} | custom-call | tf_op jit(solution)/shard_map/pallas_call | solution.py:202
  108.6 5.8 %collective-permute-done.10.refs_2_ = bf16[256,2048]{1,0:T(8,128)(2,1)S(1)} collective-permute-done((bf16[256,2048]{1,0:T(8,128)(2,1)S(1)}, bf16[256,2048]{1,0:T(8,128)(2,1)S(1)}, u32[]{:S(2)}, u32[]{:S(2)}) %collective-permute-start.10) | collective-permute-done | bytes 1048608 | tf_op jit(solution)/shard_map/ppermute | solution.py:21
  114.4 0.0 collective-permute-done.11.refs_3_
  114.4 2.5 %collective-permute-start.12 = (bf16[256,2048]{1,0:T(8,128)(2,1)S(1)}, bf16[256,2048]{1,0:T(8,128)(2,1)S(1)}, u32[]{:S(2)}, u32[]{:S(2)}) collective-permute-start(bf16[256,2048]{1,0:T(8,128)(2,1)S(1)} %collective-permute-done.10.refs_2_), channel_id=1, source_target_pairs={{4,8},{12,0},{5,9},{13,1},{6,10},{14,2},{7,11},{15,3},{20,24},{28,... | collective-permute-start | bytes 3145736 | tf_op jit(solution)/shard_map/ppermute | solution.py:30
  116.9 0.0 collective-permute-done.13.refs_1_
  116.9 1.3 collective-permute-start.14
  118.2 14.3 %collective-permute-done.9.refs_0_.refs_1_ = bf16[256,2048]{1,0:T(8,128)(2,1)S(1)} collective-permute-done((bf16[256,2048]{1,0:T(8,128)(2,1)S(1)}, bf16[256,2048]{1,0:T(8,128)(2,1)S(1)}, u32[]{:S(2)}, u32[]{:S(2)}) %collective-permute-start.9) | collective-permute-done | bytes 1048608 | tf_op jit(solution)/shard_map/ppermute | solution.py:21
  132.5 0.0 collective-permute-done.12.refs_4_
  132.5 0.7 collective-permute-start.15
  133.2 2.5 %collective-permute-start.16 = (bf16[256,2048]{1,0:T(8,128)(2,1)S(1)}, bf16[256,2048]{1,0:T(8,128)(2,1)S(1)}, u32[]{:S(2)}, u32[]{:S(2)}) collective-permute-start(bf16[256,2048]{1,0:T(8,128)(2,1)S(1)} %collective-permute-done.9.refs_0_.refs_1_), channel_id=1, source_target_pairs={{4,8},{12,0},{5,9},{13,1},{6,10},{14,2},{7,11},{15,3},{20,24},{28,... | collective-permute-start | bytes 3145736 | tf_op jit(solution)/shard_map/ppermute | solution.py:30
  135.7 0.0 collective-permute-done.14.refs_5_
  135.8 9.2 %shard_map.40 = (f32[512,2048]{1,0:T(8,128)S(1)}, f32[512,2048]{1,0:T(8,128)S(1)}, f32[8,128]{1,0:T(8,128)S(1)}) custom-call(f32[4]{0:T(128)S(1)} %copy-done.3, f32[4]{0:T(128)S(1)} %collective-permute-done.energy_part, f32[1,128]{1,0:T(1,128)S(1)} %dynamic-slice_bitcast_fusion.virt_rows, ...), custom_call_target="tpu_custom_call", output_to_operand_aliasing={{0}: (13, {}), {1}: (14, {})} | custom-call | tf_op jit(solution)/shard_map/pallas_call | solution.py:202
  144.9 0.0 collective-permute-done.15.refs_0_
  144.9 2.5 %collective-permute-done.16.refs_1_.refs_2_ = bf16[256,2048]{1,0:T(8,128)(2,1)S(1)} collective-permute-done((bf16[256,2048]{1,0:T(8,128)(2,1)S(1)}, bf16[256,2048]{1,0:T(8,128)(2,1)S(1)}, u32[]{:S(2)}, u32[]{:S(2)}) %collective-permute-start.16) | collective-permute-done | bytes 1048608 | tf_op jit(solution)/shard_map/ppermute | solution.py:30
  147.4 3.0 %shard_map.41 = (bf16[512,2048]{1,0:T(8,128)(2,1)S(1)}, f32[8,128]{1,0:T(8,128)S(1)}) custom-call(f32[4]{0:T(128)S(1)} %copy-done.3, f32[4]{0:T(128)S(1)} %collective-permute-done.energy_part, f32[1,128]{1,0:T(1,128)S(1)} %dynamic-slice_bitcast_fusion.virt_rows, f32[512,1]{1,0:T(8,128)S(1)} %copy.17.virt_column, f32[8,128]{1,0:T(8,128)S(1)} %get-tuple-element.58.after, ...), custom_call_target="tpu_custom_call" | custom-call | tf_op jit(solution)/shard_map/pallas_call | solution.py:202
  150.4 1.3 collective-permute-start.17
  151.7 1.3 collective-permute-start.18
  153.0 2.4 %collective-permute-done.17.refs_1_.refs_3_ = bf16[256,2048]{1,0:T(8,128)(2,1)S(1)} collective-permute-done((bf16[256,2048]{1,0:T(8,128)(2,1)S(1)}, bf16[256,2048]{1,0:T(8,128)(2,1)S(1)}, u32[]{:S(2)}, u32[]{:S(2)}) %collective-permute-start.17) | collective-permute-done | bytes 1048608 | tf_op jit(solution)/shard_map/ppermute | solution.py:30
  155.3 3.0 %shard_map.42 = (bf16[512,2048]{1,0:T(8,128)(2,1)S(1)}, f32[8,128]{1,0:T(8,128)S(1)}) custom-call(f32[4]{0:T(128)S(1)} %copy-done.3, f32[4]{0:T(128)S(1)} %collective-permute-done.energy_part, f32[1,128]{1,0:T(1,128)S(1)} %dynamic-slice_bitcast_fusion.virt_rows, f32[512,1]{1,0:T(8,128)S(1)} %copy.17.virt_column, f32[8,128]{1,0:T(8,128)S(1)} %get-tuple-element.62.after, ...), custom_call_target="tpu_custom_call" | custom-call | tf_op jit(solution)/shard_map/pallas_call | solution.py:202
  158.3 2.2 %collective-permute-start.19 = (bf16[512,2048]{1,0:T(8,128)(2,1)S(1)}, bf16[512,2048]{1,0:T(8,128)(2,1)S(1)}, u32[]{:S(2)}, u32[]{:S(2)}) collective-permute-start(bf16[512,2048]{1,0:T(8,128)(2,1)S(1)} %get-tuple-element.68), channel_id=1, source_target_pairs={{4,0},{12,8},{5,1},{13,9},{6,2},{14,10},{7,3},{15,11},{20,16},{28,... | collective-permute-start | bytes 6291464 | tf_op jit(solution)/shard_map/ppermute | solution.py:30
  160.5 4.4 %shard_map.43 = (f32[512,2048]{1,0:T(8,128)S(1)}, f32[8,128]{1,0:T(8,128)}) custom-call(f32[4]{0:T(128)S(1)} %copy-done.3, f32[4]{0:T(128)S(1)} %collective-permute-done.energy_part, f32[1,128]{1,0:T(1,128)S(1)} %dynamic-slice_bitcast_fusion.virt_rows, f32[512,1]{1,0:T(8,128)S(1)} %copy.17.virt_column, ...), custom_call_target="tpu_custom_call", output_to_operand_aliasing={{0}: (11, {})} | custom-call | tf_op jit(solution)/shard_map/pallas_call | solution.py:202
  164.9 14.8 %collective-permute-done.18.refs_0_ = bf16[512,2048]{1,0:T(8,128)(2,1)S(1)} collective-permute-done((bf16[512,2048]{1,0:T(8,128)(2,1)S(1)}, bf16[512,2048]{1,0:T(8,128)(2,1)S(1)}, u32[]{:S(2)}, u32[]{:S(2)}) %collective-permute-start.18) | collective-permute-done | bytes 2097184 | tf_op jit(solution)/shard_map/ppermute | solution.py:30
  179.7 0.0 collective-permute-done.19.refs_1_
  179.7 1.5 shard_map.44
Async XLA Ops:
  0.0 46.8 %copy-start = (bf16[4,128,2048]{2,1,0:T(8,128)(2,1)S(1)}, bf16[4,128,2048]{2,1,0:T(8,128)(2,1)}, u32[]{:S(2)}) copy-start(bf16[4,128,2048]{2,1,0:T(8,128)(2,1)} %param.3) | copy-start | bytes 6291460
  0.0 34.7 %copy-start.3 = (f32[4]{0:T(128)S(1)}, f32[4]{0:T(128)}, u32[]{:S(2)}) copy-start(f32[4]{0:T(128)} %energy_own.13) | copy-start | bytes 52
  0.0 34.7 %copy-start.4 = (f32[512]{0:T(512)S(1)}, f32[512]{0:T(512)}, u32[]{:S(2)}) copy-start(f32[512]{0:T(512)} %param.5) | copy-start | bytes 6148
  0.0 32.4 %collective-permute-start.2 = (bf16[512,2048]{1,0:T(8,128)(2,1)}, bf16[512,2048]{1,0:T(8,128)(2,1)S(1)}, u32[]{:S(2)}, u32[]{:S(2)}) collective-permute-start(bf16[512,2048]{1,0:T(8,128)(2,1)} %bitcast.7), channel_id=1, source_target_pairs={{0,4},{4,8},{8,12},{12,0},{1,5},{5,9},{9,13},{13,1},{2,6},{6,10},{... | collective-permute-start | bytes 6291464 | tf_op jit(solution)/shard_map/ppermute | solution.py:16
  5.4 27.0 %collective-permute-start.1 = (bf16[256,2048]{1,0:T(8,128)(2,1)S(1)}, bf16[256,2048]{1,0:T(8,128)(2,1)}, u32[]{:S(2)}, u32[]{:S(2)}) collective-permute-start(bf16[256,2048]{1,0:T(8,128)(2,1)S(1)} %bitcast.16), channel_id=1, source_target_pairs={{0,1},{1,2},{2,3},{3,0},{4,5},{5,6},{6,7},{7,4},{8,9},{9,10},{10,1... | collective-permute-start | bytes 3145736 | tf_op jit(solution)/shard_map/ppermute | solution.py:16
  6.7 49.7 %collective-permute-start.4 = (bf16[256,2048]{1,0:T(8,128)(2,1)}, bf16[256,2048]{1,0:T(8,128)(2,1)S(1)}, u32[]{:S(2)}, u32[]{:S(2)}) collective-permute-start(bf16[256,2048]{1,0:T(8,128)(2,1)} %bitcast.3), channel_id=1, source_target_pairs={{0,1},{1,2},{2,3},{3,0},{4,5},{5,6},{6,7},{7,4},{8,9},{9,10},{10,1... | collective-permute-start | bytes 3145736 | tf_op jit(solution)/shard_map/ppermute | solution.py:16
  32.4 1.3 copy-start.1
  33.7 22.7 %collective-permute-start.5 = (bf16[256,2048]{1,0:T(8,128)(2,1)}, bf16[256,2048]{1,0:T(8,128)(2,1)}, u32[]{:S(2)}, u32[]{:S(2)}) collective-permute-start(bf16[256,2048]{1,0:T(8,128)(2,1)} %collective-permute-done.1.refs_0_), channel_id=1, source_target_pairs={{0,4},{4,8},{8,12},{12,0},{1,5},{5,9},{9,13},{13,1},{2,6},{6,10},{... | collective-permute-start | bytes 3145736 | tf_op jit(solution)/shard_map/ppermute | solution.py:16
  34.7 12.1 %collective-permute-start = (f32[4]{0:T(128)S(1)}, f32[4]{0:T(128)S(1)}, u32[]{:S(2)}, u32[]{:S(2)}) collective-permute-start(f32[4]{0:T(128)S(1)} %copy-done.3), channel_id=1, source_target_pairs={{0,4},{4,8},{8,12},{12,0},{1,5},{5,9},{9,13},{13,1},{2,6},{6,10},{... | collective-permute-start | bytes 56 | tf_op jit(solution)/shard_map/ppermute | solution.py:16
  35.0 42.4 %collective-permute-start.3 = (bf16[256,2048]{1,0:T(8,128)(2,1)}, bf16[256,2048]{1,0:T(8,128)(2,1)S(1)}, u32[]{:S(2)}, u32[]{:S(2)}) collective-permute-start(bf16[256,2048]{1,0:T(8,128)(2,1)} %collective-permute-done.1.refs_0_), channel_id=1, source_target_pairs={{0,1},{1,2},{2,3},{3,0},{4,5},{5,6},{6,7},{7,4},{8,9},{9,10},{10,1... | collective-permute-start | bytes 3145736 | tf_op jit(solution)/shard_map/ppermute | solution.py:16
  46.8 1.6 copy-start.2
  56.4 20.9 %collective-permute-start.6 = (bf16[256,2048]{1,0:T(8,128)(2,1)S(1)}, bf16[256,2048]{1,0:T(8,128)(2,1)S(1)}, u32[]{:S(2)}, u32[]{:S(2)}) collective-permute-start(bf16[256,2048]{1,0:T(8,128)(2,1)S(1)} %collective-permute-done.4.refs_1_), channel_id=1, source_target_pairs={{0,4},{4,8},{8,12},{12,0},{1,5},{5,9},{9,13},{13,1},{2,6},{6,10},{... | collective-permute-start | bytes 3145736 | tf_op jit(solution)/shard_map/ppermute | solution.py:16
  59.0 39.8 %collective-permute-start.7 = (bf16[256,2048]{1,0:T(8,128)(2,1)S(1)}, bf16[256,2048]{1,0:T(8,128)(2,1)S(1)}, u32[]{:S(2)}, u32[]{:S(2)}) collective-permute-start(bf16[256,2048]{1,0:T(8,128)(2,1)S(1)} %collective-permute-done.4.refs_1_), channel_id=1, source_target_pairs={{0,1},{1,2},{2,3},{3,0},{4,5},{5,6},{6,7},{7,4},{8,9},{9,10},{10,1... | collective-permute-start | bytes 3145736 | tf_op jit(solution)/shard_map/ppermute | solution.py:16
  77.3 21.4 %collective-permute-start.8 = (bf16[256,2048]{1,0:T(8,128)(2,1)S(1)}, bf16[256,2048]{1,0:T(8,128)(2,1)S(1)}, u32[]{:S(2)}, u32[]{:S(2)}) collective-permute-start(bf16[256,2048]{1,0:T(8,128)(2,1)S(1)} %collective-permute-done.3.refs_0_), channel_id=1, source_target_pairs={{0,4},{4,8},{8,12},{12,0},{1,5},{5,9},{9,13},{13,1},{2,6},{6,10},{... | collective-permute-start | bytes 3145736 | tf_op jit(solution)/shard_map/ppermute | solution.py:16
  78.2 36.2 %collective-permute-start.10 = (bf16[256,2048]{1,0:T(8,128)(2,1)S(1)}, bf16[256,2048]{1,0:T(8,128)(2,1)S(1)}, u32[]{:S(2)}, u32[]{:S(2)}) collective-permute-start(bf16[256,2048]{1,0:T(8,128)(2,1)S(1)} %collective-permute-done.3.refs_0_), channel_id=1, source_target_pairs={{4,5},{5,6},{6,7},{7,4},{12,13},{13,14},{14,15},{15,12},{20,21},{2... | collective-permute-start | bytes 3145736 | tf_op jit(solution)/shard_map/ppermute | solution.py:21
  98.8 15.6 %collective-permute-start.11 = (bf16[256,2048]{1,0:T(8,128)(2,1)S(1)}, bf16[256,2048]{1,0:T(8,128)(2,1)S(1)}, u32[]{:S(2)}, u32[]{:S(2)}) collective-permute-start(bf16[256,2048]{1,0:T(8,128)(2,1)S(1)} %collective-permute-done.7.refs_0_), channel_id=1, source_target_pairs={{0,4},{4,8},{8,12},{12,0},{1,5},{5,9},{9,13},{13,1},{2,6},{6,10},{... | collective-permute-start | bytes 3145736 | tf_op jit(solution)/shard_map/ppermute | solution.py:16
  100.7 16.2 %collective-permute-start.13 = (bf16[256,2048]{1,0:T(8,128)(2,1)S(1)}, bf16[256,2048]{1,0:T(8,128)(2,1)S(1)}, u32[]{:S(2)}, u32[]{:S(2)}) collective-permute-start(bf16[256,2048]{1,0:T(8,128)(2,1)S(1)} %collective-permute-done.3.refs_0_), channel_id=1, source_target_pairs={{0,1},{1,2},{2,3},{3,0},{8,9},{9,10},{10,11},{11,8},{16,17},{17,18... | collective-permute-start | bytes 3145736 | tf_op jit(solution)/shard_map/ppermute | solution.py:21
  101.4 31.1 %collective-permute-start.9 = (bf16[256,2048]{1,0:T(8,128)(2,1)S(1)}, bf16[256,2048]{1,0:T(8,128)(2,1)S(1)}, u32[]{:S(2)}, u32[]{:S(2)}) collective-permute-start(bf16[256,2048]{1,0:T(8,128)(2,1)S(1)} %collective-permute-done.7.refs_0_), channel_id=1, source_target_pairs={{4,5},{5,6},{6,7},{7,4},{12,13},{13,14},{14,15},{15,12},{20,21},{2... | collective-permute-start | bytes 3145736 | tf_op jit(solution)/shard_map/ppermute | solution.py:21
  114.4 18.1 %collective-permute-start.12 = (bf16[256,2048]{1,0:T(8,128)(2,1)S(1)}, bf16[256,2048]{1,0:T(8,128)(2,1)S(1)}, u32[]{:S(2)}, u32[]{:S(2)}) collective-permute-start(bf16[256,2048]{1,0:T(8,128)(2,1)S(1)} %collective-permute-done.10.refs_2_), channel_id=1, source_target_pairs={{4,8},{12,0},{5,9},{13,1},{6,10},{14,2},{7,11},{15,3},{20,24},{28,... | collective-permute-start | bytes 3145736 | tf_op jit(solution)/shard_map/ppermute | solution.py:30
  116.9 18.9 %collective-permute-start.14 = (bf16[256,2048]{1,0:T(8,128)(2,1)S(1)}, bf16[256,2048]{1,0:T(8,128)(2,1)S(1)}, u32[]{:S(2)}, u32[]{:S(2)}) collective-permute-start(bf16[256,2048]{1,0:T(8,128)(2,1)S(1)} %collective-permute-done.13.refs_1_), channel_id=1, source_target_pairs={{0,4},{8,12},{1,5},{9,13},{2,6},{10,14},{3,7},{11,15},{16,20},{24,... | collective-permute-start | bytes 3145736 | tf_op jit(solution)/shard_map/ppermute | solution.py:30
  132.5 12.5 %collective-permute-start.15 = (bf16[256,2048]{1,0:T(8,128)(2,1)S(1)}, bf16[256,2048]{1,0:T(8,128)(2,1)S(1)}, u32[]{:S(2)}, u32[]{:S(2)}) collective-permute-start(bf16[256,2048]{1,0:T(8,128)(2,1)S(1)} %collective-permute-done.7.refs_0_), channel_id=1, source_target_pairs={{0,1},{1,2},{2,3},{3,0},{8,9},{9,10},{10,11},{11,8},{16,17},{17,18... | collective-permute-start | bytes 3145736 | tf_op jit(solution)/shard_map/ppermute | solution.py:21
  133.2 14.2 %collective-permute-start.16 = (bf16[256,2048]{1,0:T(8,128)(2,1)S(1)}, bf16[256,2048]{1,0:T(8,128)(2,1)S(1)}, u32[]{:S(2)}, u32[]{:S(2)}) collective-permute-start(bf16[256,2048]{1,0:T(8,128)(2,1)S(1)} %collective-permute-done.9.refs_0_.refs_1_), channel_id=1, source_target_pairs={{4,8},{12,0},{5,9},{13,1},{6,10},{14,2},{7,11},{15,3},{20,24},{28,... | collective-permute-start | bytes 3145736 | tf_op jit(solution)/shard_map/ppermute | solution.py:30
  150.4 5.0 %collective-permute-start.17 = (bf16[256,2048]{1,0:T(8,128)(2,1)S(1)}, bf16[256,2048]{1,0:T(8,128)(2,1)S(1)}, u32[]{:S(2)}, u32[]{:S(2)}) collective-permute-start(bf16[256,2048]{1,0:T(8,128)(2,1)S(1)} %collective-permute-done.15.refs_0_), channel_id=1, source_target_pairs={{0,4},{8,12},{1,5},{9,13},{2,6},{10,14},{3,7},{11,15},{16,20},{24,... | collective-permute-start | bytes 3145736 | tf_op jit(solution)/shard_map/ppermute | solution.py:30
  151.7 28.0 %collective-permute-start.18 = (bf16[512,2048]{1,0:T(8,128)(2,1)S(1)}, bf16[512,2048]{1,0:T(8,128)(2,1)S(1)}, u32[]{:S(2)}, u32[]{:S(2)}) collective-permute-start(bf16[512,2048]{1,0:T(8,128)(2,1)S(1)} %get-tuple-element.67), channel_id=1, source_target_pairs={{0,12},{8,4},{1,13},{9,5},{2,14},{10,6},{3,15},{11,7},{16,28},{24,... | collective-permute-start | bytes 6291464 | tf_op jit(solution)/shard_map/ppermute | solution.py:30
  158.3 21.4 %collective-permute-start.19 = (bf16[512,2048]{1,0:T(8,128)(2,1)S(1)}, bf16[512,2048]{1,0:T(8,128)(2,1)S(1)}, u32[]{:S(2)}, u32[]{:S(2)}) collective-permute-start(bf16[512,2048]{1,0:T(8,128)(2,1)S(1)} %get-tuple-element.68), channel_id=1, source_target_pairs={{4,0},{12,8},{5,1},{13,9},{6,2},{14,10},{7,3},{15,11},{20,16},{28,... | collective-permute-start | bytes 6291464 | tf_op jit(solution)/shard_map/ppermute | solution.py:30
